TPU v7x, 128 devices: a whole 4x4x4 slice. The times are simulated.
128 devices in a mesh: expert: 8 (over z, y_hi), tok: 16 (over y_lo, x, core).
Axes of the slice: x: 4, y: 4 (y_hi: 2, y_lo: 2; y = y_hi * 2 + y_lo), z: 4, core: 2. Of those that a mesh axis runs over, the one named last changes fastest.
Arguments:
- x_in: bfloat16 [2048, 8192], P('tok', 'expert'), may hold values from -6 to 6
- conv_w: float32 [4, 8192], P(None, 'expert'), may hold values from -3 to 3
- b_proj: bfloat16 [2048, 128], P('tok'), may hold values from -0.0234375 to 0.0234375
- c_proj: bfloat16 [2048, 128], P('tok'), may hold values from -6 to 6
- log_decay: float32 [2048, 128], P('tok', 'expert'), may hold values from -1 to 0
- d_skip: float32 [128], P('expert'), may hold values from 0.5 to 1.5
- w_out: bfloat16 [8192, 4096], P('expert', 'tok'), may hold values from -0.0625 to 0.0625
- norm_gain: float32 [4096], replicated, may hold values from 0.5 to 2
- w_router: bfloat16 [4096, 8], replicated, may hold values from -0.09375 to 0.09375
- w_expert: bfloat16 [8, 3, 4096, 12288], P('expert', None, None, 'tok'), may hold values from -0.09375 to 0.09375
- route_ids: int32 [16, 128, 2], P('tok', 'expert'), may hold values from 0 to 7, as said below
Outputs:
- layer_out: bfloat16 [16, 128, 4096], P('tok', 'expert')
Inputs may be any that keep to these rules, and one draw needn't show every extreme that they name: `route_ids`: each row names two different experts. Among the 16 rows that one device holds, one expert, the same on every device, is named by exactly 10 rows, and every other expert by at most 4 rows; some expert other than that one reaches 4 on every device.
All inputs are finite; a program needn't handle non-finite values.
Results may differ from a plain program's by a relative error of at most 0.034.
Values may be sent and summed in bfloat16 or wider, within the bound.
A program may use at most 192 MiB of HBM per device.

v0:
```python
import jax
import jax.numpy as jnp
from jax import lax
from jax.sharding import PartitionSpec as P

N_STATE = 128
CONV = 4
HEAD = 64
BLOCK = 128


highest = lax.Precision.HIGHEST


def from_behind(value, axis, steps):
    count = lax.axis_size(axis)
    first, last = (max(0, -steps), min(count, count - steps))
    return lax.ppermute(value, axis, [(source, source + steps) for source in range(first, last)])


def prefix_2(x, axis, join, neutral):
    place = lax.axis_index(axis)
    gathered = jax.tree.map(
        lambda a, kind: lax.all_gather(a.astype(kind), axis),
        x,
        jax.tree.map(lambda a: jnp.bfloat16 if a.dtype == jnp.float32 else a.dtype, x),
    )
    state = jax.tree.map(lambda a, e: jnp.zeros_like(a) + jnp.asarray(e, a.dtype), x, neutral)

    def one(step, state):
        return join(
            state,
            jax.tree.map(
                lambda a, own: lax.dynamic_index_in_dim(a, step, 0, False).astype(own.dtype),
                gathered,
                x,
            ),
        )

    return lax.fori_loop(0, place, one, state)


def block_terms(x_block, b_block, c_block, decay_block):
    length = decay_block.shape[0]
    cumulative = jnp.cumsum(decay_block, axis=0).T
    spread = cumulative[:, :, None] - cumulative[:, None, :]
    lower_mask = (
        jnp.arange(length, dtype=jnp.int32)[:, None] >= jnp.arange(length, dtype=jnp.int32)[None, :]
    )
    decay_matrix = jnp.where(
        lower_mask[None], jnp.exp(jnp.where(lower_mask[None], spread, 0.0)), 0.0
    )
    scores = jnp.einsum("in,jn->ij", c_block, b_block, precision=highest)
    y_local = jnp.einsum("hij,jhp->ihp", decay_matrix * scores[None], x_block, precision=highest)
    tail_decay = jnp.exp(cumulative[:, -1:] - cumulative)
    state_block = jnp.einsum("hj,jhp,jn->hpn", tail_decay, x_block, b_block, precision=highest)
    total_decay = jnp.exp(cumulative[:, -1])
    entry_decay = jnp.exp(cumulative)
    return (y_local, state_block, total_decay, entry_decay)


def combine_states(earlier, following):
    earlier_decay, earlier_state = earlier
    following_decay, following_state = following
    return (
        earlier_decay * following_decay,
        following_decay[:, None, None] * earlier_state + following_state,
    )


def expert_partial(tokens_in, weights):
    gate_value = jnp.dot(tokens_in, weights[0], preferred_element_type=jnp.float32)
    up_value = jnp.dot(tokens_in, weights[1], preferred_element_type=jnp.float32)
    active = (jax.nn.silu(gate_value) * up_value).astype(jnp.bfloat16)
    return lax.dot_general(
        active, weights[2], (((1,), (1,)), ((), ())), preferred_element_type=jnp.float32
    )


def slot_table(routed, capacity):
    token_count, per_token, experts = routed.shape
    flat_hits = routed.reshape(token_count * per_token, experts).astype(jnp.int32)
    before = jnp.cumsum(flat_hits, axis=0) - flat_hits
    slot_rank = jnp.sum(before * flat_hits, axis=1)
    present = jnp.sum(flat_hits, axis=1)
    slot_hit = (jnp.arange(capacity, dtype=jnp.int32)[None, :] == slot_rank[:, None]).astype(
        jnp.int32
    ) * present[:, None]
    placement = flat_hits[:, :, None] * slot_hit[:, None, :]
    return placement.reshape(token_count, per_token, experts * capacity)


def on_device(
    x_in, conv_w, b_proj, c_proj, log_decay, d_skip, w_out, norm_gain, w_router, w_expert, route_ids
):
    seq_rows, chan_dev = x_in.shape
    tail_rows = x_in[seq_rows - (CONV - 1) :]
    earlier_rows = from_behind(tail_rows, "tok", 1)
    extended = jnp.concatenate([earlier_rows, x_in], axis=0).astype(jnp.float32)
    conv_sum = conv_w[0] * extended[0:seq_rows]
    for offset in range(1, CONV):
        conv_sum = conv_sum + conv_w[offset] * extended[offset : offset + seq_rows]
    conv_out = jax.nn.silu(conv_sum)
    heads_dev = chan_dev // HEAD
    blocks = seq_rows // BLOCK
    x_heads = conv_out.reshape(blocks, BLOCK, heads_dev, HEAD)
    b_blocks = b_proj.astype(jnp.float32).reshape(blocks, BLOCK, N_STATE)
    c_blocks = c_proj.astype(jnp.float32).reshape(blocks, BLOCK, N_STATE)
    decay_blocks = log_decay.reshape(blocks, BLOCK, heads_dev)

    def local_step(carry_pair, inputs):
        carry_decay, carry_state = carry_pair
        y_local, state_block, total_decay, entry_decay = block_terms(*inputs)
        advanced = (
            carry_decay * total_decay,
            total_decay[:, None, None] * carry_state + state_block,
        )
        return (advanced, (y_local, entry_decay, carry_decay, carry_state))

    identity = (
        jnp.ones((heads_dev,), jnp.float32),
        jnp.zeros((heads_dev, HEAD, N_STATE), jnp.float32),
    )
    device_total, stacked = lax.scan(
        local_step, identity, (x_heads, b_blocks, c_blocks, decay_blocks)
    )
    y_locals, entry_decays, lead_decays, lead_states = stacked
    prefix = prefix_2(device_total, "tok", combine_states, identity)
    incoming = lead_decays[:, :, None, None] * prefix[1][None] + lead_states
    y_carry = jnp.einsum("bhi,bin,bhpn->bihp", entry_decays, c_blocks, incoming, precision=highest)
    mixed = (y_locals + y_carry).reshape(seq_rows, heads_dev, HEAD) + d_skip[
        None, :, None
    ] * conv_out.reshape(seq_rows, heads_dev, HEAD)
    scan_out = mixed.reshape(seq_rows, chan_dev).astype(jnp.bfloat16)
    terms = jnp.dot(
        scan_out,
        lax.all_gather(w_out, "tok", axis=1, tiled=True),
        preferred_element_type=jnp.float32,
    )
    hidden = lax.psum_scatter(terms.astype(jnp.bfloat16), "expert", scatter_dimension=0, tiled=True)
    hidden_f = hidden.astype(jnp.float32)
    mean_square = jnp.mean(hidden_f * hidden_f, axis=-1, keepdims=True)
    normed = (hidden_f * lax.rsqrt(mean_square + 1e-05) * norm_gain).astype(jnp.bfloat16)
    logits = jnp.dot(normed, w_router, preferred_element_type=jnp.float32)
    tokens_dev, model_width = normed.shape
    experts = w_router.shape[1]
    route = route_ids[0]
    chosen = route[:, :, None] == jnp.arange(experts, dtype=jnp.int32)[None, None, :]
    picked = jnp.sum(jnp.where(chosen, logits[:, None, :], 0.0), axis=2)
    sigmas = jax.nn.sigmoid(picked)
    gates = sigmas / jnp.sum(sigmas, axis=1, keepdims=True)
    hot_slots = 5 * tokens_dev // 8
    placement = slot_table(chosen, hot_slots)
    place_all = jnp.sum(placement, axis=1).astype(jnp.bfloat16)
    outgoing = lax.dot_general(
        place_all, normed, (((0,), (0,)), ((), ())), preferred_element_type=jnp.float32
    ).astype(jnp.bfloat16)
    received = lax.all_to_all(
        outgoing.reshape(experts, hot_slots, model_width),
        "expert",
        split_axis=0,
        concat_axis=0,
        tiled=True,
    )
    expert_in = received.reshape(experts * hot_slots, model_width)
    part_out = expert_partial(lax.all_gather(expert_in, "tok", axis=0, tiled=True), w_expert[0])
    partials = lax.optimization_barrier(part_out.astype(jnp.bfloat16)).astype(jnp.float32)
    summed = lax.psum_scatter(
        partials.astype(jnp.bfloat16), "tok", scatter_dimension=0, tiled=True
    ).astype(jnp.float32)
    returned = lax.all_to_all(
        summed.reshape(experts, hot_slots, model_width).astype(jnp.bfloat16),
        "expert",
        split_axis=0,
        concat_axis=0,
        tiled=True,
    ).astype(jnp.float32)
    flat_back = returned.reshape(experts * hot_slots, model_width)
    moe_sum = jnp.zeros((tokens_dev, model_width), jnp.float32)
    for position in range(2):
        pick_table = placement[:, position].astype(jnp.float32)
        gathered = jnp.dot(pick_table, flat_back, precision=highest)
        moe_sum = moe_sum + gates[:, position : position + 1] * gathered
    layer_out = (hidden_f + moe_sum).astype(jnp.bfloat16)
    return layer_out.reshape(1, tokens_dev, model_width)


def solution(mesh):
    placed = (
        P("tok", "expert"),
        P(None, "expert"),
        P("tok", None),
        P("tok", None),
        P("tok", "expert"),
        P("expert"),
        P("expert", "tok"),
        P(),
        P(),
        P("expert", None, None, "tok"),
        P("tok", "expert", None),
    )
    return jax.shard_map(
        on_device, mesh=mesh, in_specs=placed, out_specs=P("tok", "expert", None), check_vma=False
    )
```

profile of v0, /device:TPU:6, one launch (start us, length us, event | category | flops | bytes accessed | tf_op | source)
XLA Modules:
  0.0 427.1 jit_solution(13875126750547528585)
XLA Ops:
  6.6 0.8 slice.57
  7.4 0.2 copy.43
  7.6 1.9 collective-permute-start
  9.5 0.9 fusion.50
  10.4 0.8 copy.45
  11.2 0.2 reduce_window_sum.23
  11.4 1.1 copy.44
  12.5 0.1 copy.49
  12.6 2.7 collective-permute-done
  15.3 0.2 maximum_convert_fusion
  15.5 1.2 divide_multiply_fusion
  16.7 1.8 fusion.20
  18.6 0.0 all-gather.6.cloned.1.call-start
  18.6 0.7 all-gather.6.cloned.1.call-update
  19.4 0.1 copy.46
  19.4 0.6 dynamic-slice.3
  20.7 0.2 dynamic-update-slice
  20.9 26.2 %all-reduce = bf16[256]{0:T(256)(128)(2,1)S(1)} all-reduce(bf16[256]{0:T(256)(128)(2,1)S(1)} %dynamic-update-slice), channel_id=2, replica_groups=mesh['expert'=8,'tok'=16] {'tok'}, use_global_device_ids=true, to_apply=%add | all-reduce | flops 256 | bytes 1024
  47.1 0.1 reshape.178
  47.3 0.1 mul.193
  47.4 0.1 mul.194
  47.5 0.1 fusion.51
  47.6 10.0 %all-gather.10.cloned.1.call-done = bf16[256,64,128]{2,1,0:T(8,128)(2,1)} async-done(((bf16[16,64,128]{2,1,0:T(8,128)(2,1)}), bf16[256,64,128]{2,1,0:T(8,128)(2,1)}) %all-gather.10.cloned.1.call-update) | async-done | bytes 4194320 | tf_op jit(solution)/shard_map/all_gather | solution.py:24
  57.6 7.0 %while.3 = (s32[]{:T(128)}, f32[16,64,128]{2,1,0:T(8,128)S(1)}, s32[]{:T(128)}, bf16[16,16]{1,0:T(8,128)(2,1)S(1)}, bf16[16,16,64,128]{3,2,1,0:T(8,128)(2,1)}, /*index=5*/s32[]{:T(128)}, s32[]{:T(128)}, s32[]{:T(128)}) while((s32[]{:T(128)}, f32[16,64,128]{2,1,0:T(8,128)S(1)}, s32[]{:T(128)}, bf16[16,16]{1,0:T(8,128)(2,1)S(1)}, ...), condition=%wide.region_2.3_spmd, body=%wide.region_1.2_spmd.sunk | while | flops 393237 | bytes 1311007 | solution.py:40
  57.7 1.1 convert_add_fusion.2
  58.8 1.1 convert_add_fusion.2
  60.0 1.1 convert_add_fusion.2
  61.2 1.1 convert_add_fusion.2
  62.3 1.1 convert_add_fusion.2
  63.5 1.1 convert_add_fusion.2
  64.6 0.4 fusion.19
  65.0 2.2 fusion.18
  67.2 1.4 fusion.29
  68.6 50.9 %all-gather.6.cloned.1.call-done = bf16[1024,4096]{1,0:T(8,128)(2,1)} async-done(((bf16[1024,256]{1,0:T(8,128)(2,1)}), bf16[1024,4096]{1,0:T(8,128)(2,1)}) %all-gather.6.cloned.1.call-update) | async-done | bytes 8388624 | tf_op jit(solution)/shard_map/all_gather | solution.py:137
  119.5 5.7 %convolution_convert_fusion.1 = bf16[128,4096]{1,0:T(8,128)(2,1)} fusion(bf16[128,1024]{0,1:T(8,128)(2,1)S(1)} %fusion.29, bf16[1024,4096]{1,0:T(8,128)(2,1)} %all-gather.6.cloned.1.call-done), kind=kOutput, calls=%fused_computation.11 | convolution fusion | flops 1074266112 | bytes 9699328 | tf_op jit(solution)/shard_map/dot_general | solution.py:135
  125.2 0.0 all-gather.8.cloned.1.call-start
  125.3 0.1 copy.50
  125.3 0.1 eq.49
  125.4 0.1 fusion.45
  125.5 0.1 reduce_window_sum.24
  125.6 0.2 select_reduce_fusion
  125.8 0.1 fusion.46
  125.8 0.1 broadcast_multiply_fusion
  125.9 0.1 mul.210
  126.1 72.5 %reduce-scatter.3.cloned.1.call-done = bf16[16,4096]{1,0:T(8,128)(2,1)} async-done(((bf16[128,4096]{1,0:T(8,128)(2,1)}), bf16[16,4096]{1,0:T(8,128)(2,1)}) %reduce-scatter.3.cloned.1.call-update) | async-done | bytes 131088 | tf_op jit(solution)/shard_map/reduce_scatter | solution.py:140
  198.6 1.0 fusion.36
  199.6 1.3 convolution_convert_fusion.2
  200.9 0.2 reshape.172
  201.1 19.9 %all_to_all.10 = bf16[8,10,4096]{2,1,0:T(8,128)(2,1)S(1)} all-to-all(bf16[8,10,4096]{2,1,0:T(8,128)(2,1)S(1)} %reshape.172), channel_id=1, replica_groups=mesh['expert'=8,'tok'=16] {'expert'}, dimensions={0} | all-to-all | bytes 1310720 | tf_op jit(solution)/shard_map/all_to_all | solution.py:158
  221.0 1.1 reshape.173
  222.1 0.2 reduce-scatter.5.cloned.1.call-start
  222.3 58.9 %all-gather.8.cloned.1.call-done = bf16[1280,4096]{1,0:T(8,128)(2,1)} async-done(((bf16[80,4096]{1,0:T(8,128)(2,1)}), bf16[1280,4096]{1,0:T(8,128)(2,1)}) %all-gather.8.cloned.1.call-update) | async-done | bytes 10485776 | tf_op jit(solution)/shard_map/all_gather | solution.py:166
  281.3 12.3 %fusion.3 = f32[1280,768]{1,0:T(8,128)S(1)} fusion(bf16[1280,4096]{1,0:T(8,128)(2,1)} %all-gather.8.cloned.1.call-done, bf16[1,3,4096,768]{3,2,1,0:T(8,128)(2,1)} %param.22), kind=kOutput, calls=%fused_computation.6 | convolution fusion | flops 8053063680 | bytes 20709376 | tf_op jit(solution)/shard_map/dot_general | solution.py:72
  293.6 11.2 %fusion.15 = bf16[1280,768]{1,0:T(8,128)(2,1)S(1)} fusion(bf16[1280,4096]{1,0:T(8,128)(2,1)S(1)} %copy-done.7, bf16[1,3,4096,768]{3,2,1,0:T(8,128)(2,1)} %param.22, f32[1280,768]{1,0:T(8,128)S(1)} %fusion.3), kind=kOutput, calls=%fused_computation.20 | convolution fusion | flops 8058961920 | bytes 22675456 | tf_op jit(solution)/shard_map/dot_general | solution.py:73
  304.8 13.4 %convolution_convert_fusion = bf16[1280,4096]{1,0:T(8,128)(2,1)} fusion(bf16[1280,768]{1,0:T(8,128)(2,1)S(1)} %fusion.15, bf16[1,3,4096,768]{3,2,1,0:T(8,128)(2,1)} %param.22), kind=kOutput, calls=%fused_computation.2 | convolution fusion | flops 8058306560 | bytes 18743296 | tf_op jit(solution)/shard_map/dot_general | solution.py:75
  318.3 0.8 copy-done.1
  319.1 0.2 fusion.43
  319.3 73.7 %reduce-scatter.5.cloned.1.call-done = bf16[80,4096]{1,0:T(8,128)(2,1)} async-done(((bf16[1280,4096]{1,0:T(8,128)(2,1)}), bf16[80,4096]{1,0:T(8,128)(2,1)}) %reduce-scatter.5.cloned.1.call-update) | async-done | bytes 655376 | tf_op jit(solution)/shard_map/reduce_scatter | solution.py:168
  393.0 2.3 convert_element_type.109
  395.3 6.9 %all-to-all-start.1 = ((bf16[8,10,4096]{2,1,0:T(8,128)(2,1)}), bf16[8,10,4096]{2,1,0:T(8,128)(2,1)S(1)}, u32[]{:S(2)}, u32[]{:S(2)}) async-start(bf16[8,10,4096]{2,1,0:T(8,128)(2,1)} %convert_element_type.109), calls=%async_computation.3 | async-start | bytes 2097152 | tf_op jit(solution)/shard_map/all_to_all | solution.py:171
  402.2 16.7 %all-to-all-done.1 = bf16[8,10,4096]{2,1,0:T(8,128)(2,1)S(1)} async-done(((bf16[8,10,4096]{2,1,0:T(8,128)(2,1)}), bf16[8,10,4096]{2,1,0:T(8,128)(2,1)S(1)}, u32[]{:S(2)}, u32[]{:S(2)}) %all-to-all-start.1) | async-done | bytes 655392 | tf_op jit(solution)/shard_map/all_to_all | solution.py:171
  418.9 0.2 reshape.174
  419.2 0.4 convolution_multiply_fusion
  419.6 1.0 fusion.11
  (43 shorter events, 0.5 us)
Async XLA Ops:
  6.5 311.7 %copy-start = (bf16[4096,8]{0,1:T(8,128)(2,1)S(1)}, bf16[4096,8]{0,1:T(8,128)(2,1)}, u32[]{:S(2)}) copy-start(bf16[4096,8]{0,1:T(8,128)(2,1)} %param.21) | copy-start | bytes 196612
  6.5 12.9 %copy-start.8 = (u32[128]{0:T(128)S(1)}, u32[128]{0:T(128)}, u32[]{:S(2)}) copy-start(u32[128]{0:T(128)} %constant.73) | copy-start | bytes 1540
  6.5 40.9 %copy-start.2 = (bf16[128,128]{1,0:T(8,128)(2,1)S(1)}, bf16[128,128]{1,0:T(8,128)(2,1)}, u32[]{:S(2)}) copy-start(bf16[128,128]{1,0:T(8,128)(2,1)} %param.15) | copy-start | bytes 98308
  6.5 40.7 %copy-start.6 = (f32[16]{0:T(128)S(1)}, f32[16]{0:T(128)}, u32[]{:S(2)}) copy-start(f32[16]{0:T(128)} %param.18) | copy-start | bytes 196
  6.5 40.9 %copy-start.3 = (bf16[128,128]{1,0:T(8,128)(2,1)S(1)}, bf16[128,128]{1,0:T(8,128)(2,1)}, u32[]{:S(2)}) copy-start(bf16[128,128]{1,0:T(8,128)(2,1)} %param.16) | copy-start | bytes 98308
  6.5 51.0 %all-gather.10.cloned.1.call-start = ((), (), s32[]{:S(2)}) async-start(), calls=%async_computation.8 | async-start | bytes 4456448 | tf_op jit(solution)/shard_map/all_gather | solution.py:24
  7.6 7.7 %collective-permute-start = (bf16[3,1024]{0,1:T(8,128)(2,1)S(1)}, bf16[3,1024]{0,1:T(8,128)(2,1)S(1)}, u32[]{:S(2)}, u32[]{:S(2)}) collective-permute-start(bf16[3,1024]{0,1:T(8,128)(2,1)S(1)} %copy.43), channel_id=1, source_target_pairs={{0,1},{1,2},{2,3},{3,4},{4,5},{5,6},{6,7},{7,8},{8,9},{9,10},{10,1... | collective-permute-start | bytes 18440 | tf_op jit(solution)/shard_map/ppermute | solution.py:18
  18.6 100.9 %all-gather.6.cloned.1.call-start = ((), (), s32[]{:S(2)}) async-start(), calls=%async_computation.4 | async-start | bytes 8912896 | tf_op jit(solution)/shard_map/all_gather | solution.py:137
  19.3 179.3 %reduce-scatter.3.cloned.1.call-start = ((), (), s32[]{:S(2)}) async-start(), calls=%async_computation.5 | async-start | bytes 1179648 | tf_op jit(solution)/shard_map/reduce_scatter | solution.py:140
  68.6 56.7 %copy-start.5 = (s32[1,16,2]{1,2,0:T(2,128)S(1)}, s32[1,16,2]{1,2,0:T(2,128)}, u32[]{:S(2)}) copy-start(s32[1,16,2]{1,2,0:T(2,128)} %param.23) | copy-start | bytes 388
  68.6 131.0 %copy-start.4 = (f32[4096]{0:T(1024)S(1)}, f32[4096]{0:T(1024)}, u32[]{:S(2)}) copy-start(f32[4096]{0:T(1024)} %param.20) | copy-start | bytes 49156
  125.2 156.1 %all-gather.8.cloned.1.call-start = ((), (), s32[]{:S(2)}) async-start(), calls=%async_computation.6 | async-start | bytes 11141120 | tf_op jit(solution)/shard_map/all_gather | solution.py:166
  222.1 170.9 %reduce-scatter.5.cloned.1.call-start = ((), (), s32[]{:S(2)}) async-start(), calls=%async_computation.7 | async-start | bytes 11141120 | tf_op jit(solution)/shard_map/reduce_scatter | solution.py:168
  281.3 12.3 %copy-start.7 = (bf16[1280,4096]{1,0:T(8,128)(2,1)S(1)}, bf16[1280,4096]{1,0:T(8,128)(2,1)}, u32[]{:S(2)}) copy-start(bf16[1280,4096]{1,0:T(8,128)(2,1)} %all-gather.8.cloned.1.call-done) | copy-start | bytes 31457284
  318.2 0.9 copy-start.1
  395.3 23.6 %all-to-all-start.1 = ((bf16[8,10,4096]{2,1,0:T(8,128)(2,1)}), bf16[8,10,4096]{2,1,0:T(8,128)(2,1)S(1)}, u32[]{:S(2)}, u32[]{:S(2)}) async-start(bf16[8,10,4096]{2,1,0:T(8,128)(2,1)} %convert_element_type.109), calls=%async_computation.3 | async-start | bytes 2097152 | tf_op jit(solution)/shard_map/all_to_all | solution.py:171
Sparse Core Ops, SparseCore 0:
  18.7 38.8 all-gather.9
  59.2 60.1 all-gather.5
  125.3 73.1 reduce-scatter.2
  222.2 58.9 all-gather.7
  318.4 74.6 reduce-scatter.4
where the time goes:
time: 430 us; the launch traced here: 427 us
  waiting for transfers between devices  286 us (67%)
  matrix products  50.1 us (12%)
  blocking collectives  46.1 us (11%)
  between operations  14.1 us (3%)
  other arithmetic  11.4 us (3%)
  local copies, waits for them, and re-layouts  10 us (2%)
  starting transfers between devices  9.17 us (2%)
    reduce_scatter x1, waiting for transfers between devices, on_device(): lax.psum_scatter(partials.astype(jnp.bfloat16), 'tok', scatter_dimension=...  73.7 us
    reduce_scatter x1, waiting for transfers between devices, on_device(): lax.psum_scatter(terms.astype(jnp.bfloat16), 'expert', scatter_dimension=...  72.5 us
    all_gather x1, waiting for transfers between devices, on_device(): lax.all_gather(expert_in, 'tok', axis=0, tiled=True)  58.9 us
    all_gather x1, waiting for transfers between devices, on_device(): lax.all_gather(w_out, 'tok', axis=1, tiled=True)  50.9 us
    unnamed x1, blocking collectives  26.2 us
    all_to_all x1, blocking collectives, on_device(): lax.all_to_all(outgoing.reshape(experts, hot_slots, model_width), 'expert...  19.9 us
    all_to_all x1, waiting for transfers between devices, on_device(): lax.all_to_all(summed.reshape(experts, hot_slots, model_width).astype(jnp...  16.7 us
    dot_general x1, matrix products, expert_partial(): lax.dot_general(active, weights[2], (((1,), (1,)), ((), ())), preferred_e...  13.4 us
  transfers between devices with their start and end apart: 7, of which 7 were waited for; matrix products, arithmetic and copies ran while one was open for 4% of the time, Pallas kernels for 0%

commit v1 on v0

v1 whole, which is shorter than its diff:
```python
import jax
import jax.numpy as jnp
from jax import lax
from jax.experimental import pallas as pl
from jax.experimental.pallas import tpu as pltpu
from jax.sharding import PartitionSpec as P

N_STATE = 128
CONV = 4
HEAD = 64
BLOCK = 128


highest = lax.Precision.HIGHEST


def from_behind(value, axis, steps):
    count = lax.axis_size(axis)
    first, last = (max(0, -steps), min(count, count - steps))
    return lax.ppermute(value, axis, [(source, source + steps) for source in range(first, last)])


def prefix_state(decay, state, axis):
    heads, head, n = state.shape
    packed = jnp.concatenate(
        [state, jnp.broadcast_to(decay[:, None, None], (heads, 8, n))], axis=1
    ).astype(jnp.bfloat16)
    gathered = lax.all_gather(packed, axis)
    place = lax.axis_index(axis)

    def one(step, held):
        item = lax.dynamic_index_in_dim(gathered, step, 0, False).astype(jnp.float32)
        return item[:, head : head + 1] * held + item[:, :head]

    return lax.fori_loop(0, place, one, jnp.zeros_like(state))


def block_terms(x_block, b_block, c_block, decay_block):
    length = decay_block.shape[0]
    ones = jnp.tril(jnp.ones((length, length), jnp.float32))
    cumulative = jnp.einsum("ij,jh->hi", ones, decay_block, precision=highest)
    spread = cumulative[:, :, None] - cumulative[:, None, :]
    lower_mask = (
        jnp.arange(length, dtype=jnp.int32)[:, None] >= jnp.arange(length, dtype=jnp.int32)[None, :]
    )
    decay_matrix = jnp.where(
        lower_mask[None], jnp.exp(jnp.where(lower_mask[None], spread, 0.0)), 0.0
    )
    scores = jnp.einsum("in,jn->ij", c_block, b_block, precision=highest)
    y_local = jnp.einsum("hij,jhp->ihp", decay_matrix * scores[None], x_block, precision=highest)
    tail_decay = jnp.exp(cumulative[:, -1:] - cumulative)
    state_block = jnp.einsum("hj,jhp,jn->hpn", tail_decay, x_block, b_block, precision=highest)
    total_decay = jnp.exp(cumulative[:, -1])
    entry_decay = jnp.exp(cumulative)
    return (y_local, state_block, total_decay, entry_decay)


MESH = pl.DeviceIdType.MESH
bf16, f32 = jnp.bfloat16, jnp.float32
NX, NE = 4, 8
ORDER = [(0, 0), (0, 1), (1, 0), (3, 0), (2, 0), (2, 1), (1, 1), (3, 1)]
PLACE = {d: i for i, d in enumerate(ORDER)}


def slot(dx, dy, dc):
    return PLACE[(dx % NX, dy % 2)] * 2 + dc % 2


class Where:
    def __init__(self):
        self.e = lax.axis_index("expert")
        self.t = lax.axis_index("tok")
        self.c = lax.rem(self.t, 2)
        self.x = lax.rem(self.t // 2, NX)
        self.y = self.t // (2 * NX)

    def tok(self, dx, dy, dc):
        return (
            lax.rem(self.y + dy, 2) * NX + lax.rem(self.x + dx, NX)
        ) * 2 + lax.rem(self.c + dc, 2)

    def tok_dev(self, dx, dy, dc):
        return {"tok": self.tok(dx, dy, dc)}

    def exp(self, k):
        return lax.rem(self.e + k, NE)


NEAR = [(0, 0, 1), (0, 1, 0), (1, 0, 0), (3, 0, 0), (2, 0, 0)]


def greet(w):
    barrier = pltpu.get_barrier_semaphore()
    for d in NEAR:
        pl.semaphore_signal(barrier, inc=1, device_id=w.tok_dev(*d), device_id_type=MESH)
    for k in range(1, NE):
        pl.semaphore_signal(barrier, inc=1, device_id={"expert": w.exp(k)}, device_id_type=MESH)
    pl.semaphore_wait(barrier, len(NEAR) + NE - 1)


class Mail:
    def __init__(self, sems):
        self.sems, self.out = sems, []

    def send(self, src, dst, rsem, dev):
        cp = pltpu.make_async_remote_copy(
            src_ref=src, dst_ref=dst, send_sem=self.sems.at[len(self.out)], recv_sem=rsem,
            device_id=dev, device_id_type=MESH,
        )
        cp.start()
        self.out.append(cp)

    def got(self, ref, rsem, dev):
        pltpu.make_async_remote_copy(
            src_ref=ref, dst_ref=ref, send_sem=self.sems.at[0], recv_sem=rsem,
            device_id=dev, device_id_type=MESH,
        ).wait_recv()

    def drain(self):
        for cp in self.out:
            cp.wait_send()


class Gather:
    def __init__(self, w, mail, view, rsems):
        self.w, self.mail, self.view, self.rsems = w, mail, view, rsems

    def put(self, frm, part, to, seen):
        s = slot(*seen)
        self.mail.send(
            self.view(slot(*frm), part), self.view(s, part), self.rsems.at[s, part],
            self.w.tok_dev(*to),
        )

    def got(self, dx, dy, dc, part):
        s = slot(dx, dy, dc)
        self.mail.got(self.view(s, part), self.rsems.at[s, part], self.w.tok_dev(0, 0, 1))

    def start(self):
        own = (0, 0, 0)
        for part in (1, 0):
            self.put(own, part, (0, 1, 0), (0, 1, 0))
        for dx in (1, 3, 2):
            self.put(own, 0, (dx, 0, 0), (-dx, 0, 0))
        for dx in (1, 3, 2):
            self.put(own, 1, (dx, 0, 0), (-dx, 0, 0))
        for part in (0, 1):
            self.put(own, part, (0, 0, 1), (0, 0, 1))

    def sib(self, dx, dy, part):
        self.put((dx, dy, 0), part, (0, 0, 1), (dx, dy, 1))

    def y_in(self):
        self.got(0, 1, 0, 1)
        for dx in (1, 3, 2):
            self.put((0, 1, 0), 1, (dx, 0, 0), (-dx, 1, 0))
        self.sib(0, 1, 1)
        self.got(0, 1, 0, 0)
        self.sib(0, 1, 0)

    def x_in(self, dx):
        self.got(dx, 0, 0, 0)
        self.put((dx, 0, 0), 0, (0, 1, 0), (dx, 1, 0))
        self.sib(dx, 0, 0)

    def x_in_late(self, dx):
        self.got(dx, 0, 0, 1)
        self.sib(dx, 0, 1)

    def far_in(self, dx):
        for part in (0, 1):
            self.got(dx, 1, 0, part)
            self.sib(dx, 1, part)

    def sib_in(self, dx, dy):
        for part in (0, 1):
            self.got(dx, dy, 1, part)


AG_SENDS = 2 + 3 + 3 + 2 + (3 + 2) + 3 * 2 + 3 + 3 * 2


def rms(hid, gain):
    ms = jnp.mean(hid * hid, axis=-1, keepdims=True)
    return hid * lax.rsqrt(ms + 1e-05) * gain


def project_kernel(
    scan_ref, wout_ref, gain_ref, hid_ref, nrm_ref, g_ref, part_ref, rec_ref, ssem, rsem, esem
):
    w = Where()
    mail = Mail(ssem)
    depth = wout_ref.shape[0]
    cut = depth * 5 // 8
    greet(w)

    def view(s, part):
        return g_ref.at[s, pl.ds(0, cut)] if part == 0 else g_ref.at[s, pl.ds(cut, depth - cut)]

    g_ref[0] = wout_ref[...]
    ag = Gather(w, mail, view, rsem)
    ag.start()
    width = wout_ref.shape[1]

    def mult(dx, dy, dc):
        cols = pl.ds(pl.multiple_of(w.tok(dx, dy, dc) * width, width), width)
        part_ref[:, cols] = jnp.dot(
            scan_ref[...], g_ref[slot(dx, dy, dc)], preferred_element_type=f32
        ).astype(bf16)

    mult(0, 0, 0)
    ag.y_in()
    for dx in (1, 3, 2):
        ag.x_in(dx)
    ag.sib_in(0, 0)
    mult(0, 0, 1)
    mult(0, 1, 0)
    for dx in (1, 3, 2):
        ag.x_in_late(dx)
        mult(dx, 0, 0)
    ag.sib_in(0, 1)
    mult(0, 1, 1)
    for dx in (1, 3, 2):
        ag.far_in(dx)
        mult(dx, 1, 0)
    for dy in (0, 1):
        for dx in (1, 3, 2):
            ag.sib_in(dx, dy)
            mult(dx, dy, 1)
    rows = hid_ref.shape[0]

    def mine(e):
        return pl.ds(pl.multiple_of(e * rows, rows), rows)

    for k in range(1, NE):
        mail.send(
            part_ref.at[mine(w.exp(k))], rec_ref.at[k - 1], esem.at[k - 1], {"expert": w.exp(k)}
        )
    total = part_ref[mine(w.e), :].astype(f32)
    for k in range(1, NE):
        mail.got(rec_ref.at[k - 1], esem.at[k - 1], {"expert": w.exp(k)})
        total = total + rec_ref[k - 1].astype(f32)
    hid_b = total.astype(bf16)
    hid_ref[...] = hid_b
    nrm_ref[...] = rms(hid_b.astype(f32), gain_ref[...]).astype(bf16)
    mail.drain()


def project(scan_out, w_out, gain, rows):
    depth, width = w_out.shape
    toks, model = scan_out.shape[0], gain.shape[1]
    vm = pl.BlockSpec(memory_space=pltpu.VMEM)
    return pl.pallas_call(
        project_kernel,
        out_shape=[jax.ShapeDtypeStruct((rows, model), bf16)] * 2,
        in_specs=[vm] * 3,
        out_specs=[vm] * 2,
        scratch_shapes=[
            pltpu.VMEM((16, depth, width), bf16),
            pltpu.VMEM((toks, model), bf16),
            pltpu.VMEM((NE - 1, rows, model), bf16),
            pltpu.SemaphoreType.DMA((AG_SENDS + NE - 1,)),
            pltpu.SemaphoreType.DMA((16, 2)),
            pltpu.SemaphoreType.DMA((NE - 1,)),
        ],
        compiler_params=pltpu.CompilerParams(
            collective_id=1, has_side_effects=True, vmem_limit_bytes=40 * 2**20
        ),
        cost_estimate=pl.CostEstimate(
            flops=2 * toks * depth * model, bytes_accessed=20 * 2**20, transcendentals=0
        ),
        name="project",
    )(scan_out, w_out, gain)


def expert_kernel(
    nrm_ref, rt_ref, hid_ref, wr_ref, we_ref, out_ref,
    wv_ref, n_ref, r_ref, g_ref, a_ref, o_ref, sib_ref, yp_ref, yq_ref, xp_ref, xq_ref,
    con_ref, rec_ref,
    lsem, ssem, nsem, tsem, gsem, bsem, psem, qsem, fsem, esem,
):
    w = Where()
    mail = Mail(ssem)
    rows, model = nrm_ref.shape
    cap = g_ref.shape[1]
    hidden = wv_ref.shape[2]
    toks = n_ref.shape[0]
    cut = model * 5 // 8
    P, Q = pl.ds(0, cut), pl.ds(cut, model - cut)
    loads = [pltpu.make_async_copy(we_ref.at[0, i], wv_ref.at[i], lsem.at[i]) for i in range(3)]
    for cp in loads:
        cp.start()
    greet(w)

    def of(e):
        return pl.ds(pl.multiple_of(e * rows, rows), rows)

    me = of(w.e)
    for k in range(1, NE):
        mail.send(rt_ref, r_ref.at[me], tsem.at[k - 1], {"expert": w.exp(k)})
        mail.send(nrm_ref, n_ref.at[me], nsem.at[k - 1], {"expert": w.exp(k)})
    n_ref[me, :] = nrm_ref[...]
    r_ref[me, :] = rt_ref[...]
    for k in range(1, NE):
        frm = of(w.exp(NE - k))
        mail.got(r_ref.at[frm], tsem.at[k - 1], {"expert": w.exp(k)})
        mail.got(n_ref.at[frm], nsem.at[k - 1], {"expert": w.exp(k)})

    ii = lax.broadcasted_iota(jnp.int32, (toks, toks), 0)
    jj = lax.broadcasted_iota(jnp.int32, (toks, toks), 1)
    eye = (ii == jj).astype(f32)
    r1 = r_ref[:, 0:1].astype(f32)
    r2 = r_ref[:, 1:2].astype(f32)
    e_f = w.e.astype(f32)
    hit = jnp.where(r1 == e_f, 1.0, 0.0) + jnp.where(r2 == e_f, 1.0, 0.0)
    rank = jnp.sum(jnp.where(ii < jj, hit, 0.0), axis=0, keepdims=True)
    hit_row = jnp.sum(hit * eye, axis=0, keepdims=True)
    want = lax.broadcasted_iota(jnp.int32, (cap, toks), 0).astype(f32)
    sel_f = jnp.where(want == rank, 1.0, 0.0) * hit_row
    sel = sel_f.astype(bf16)
    for b in range(4):
        cols = pl.ds(b * (model // 4), model // 4)
        g_ref[0, :, cols] = jnp.dot(sel, n_ref[:, cols], preferred_element_type=f32).astype(bf16)

    def view(s, part):
        return g_ref.at[s, :, Q if part else P]

    ag = Gather(w, mail, view, gsem)
    ag.start()

    logits = jnp.dot(n_ref[...], wr_ref[...], preferred_element_type=f32)
    lane = lax.broadcasted_iota(jnp.int32, logits.shape, 1).astype(f32)
    s1 = jax.nn.sigmoid(jnp.sum(jnp.where(lane == r1, logits, 0.0), axis=1, keepdims=True))
    s2 = jax.nn.sigmoid(jnp.sum(jnp.where(lane == r2, logits, 0.0), axis=1, keepdims=True))
    gate = jnp.where(r1 == e_f, s1, s2) / (s1 + s2)
    gate_row = jnp.sum(gate * eye, axis=0, keepdims=True)
    gate_col = jnp.sum(sel_f * gate_row, axis=1, keepdims=True)

    def compute(group):
        xs = pl.ds(group * 4, 4)
        tile = 256

        @pl.loop(0, hidden // tile)
        def _(i):
            cols = pl.ds(pl.multiple_of(i * tile, tile), tile)
            xg = g_ref[xs].reshape(4 * cap, model)
            gv = jnp.dot(xg, wv_ref[0, :, cols], preferred_element_type=f32)
            uv = jnp.dot(xg, wv_ref[1, :, cols], preferred_element_type=f32)
            a_ref[:, cols] = (gv / (1.0 + jnp.exp(-gv)) * uv).astype(bf16)

        if group == 0:
            loads[2].wait()

        @pl.loop(0, model // tile)
        def _(i):
            cols = pl.ds(pl.multiple_of(i * tile, tile), tile)
            o = lax.dot_general(
                a_ref[...], wv_ref[2, cols, :], (((1,), (1,)), ((), ())), preferred_element_type=f32
            )
            o_ref[xs, :, cols] = o.astype(bf16).reshape(4, cap, tile)

    def add(dst, cols, *srcs):
        @pl.loop(0, cap // 16)
        def _(i):
            r = pl.ds(pl.multiple_of(i * 16, 16), 16)
            v = o_ref[dst, r, cols].astype(f32)
            for src in srcs:
                v = v + src(r).astype(f32)
            o_ref[dst, r, cols] = v.astype(bf16)

    def pair_out(group):
        for p in (0, 1):
            i = group * 2 + p
            mail.send(o_ref.at[i * 2 + 1], sib_ref.at[i], bsem.at[i], w.tok_dev(0, 0, 1))

    def pair_in(group):
        for p in (0, 1):
            i = group * 2 + p
            dx, dy = ORDER[i]
            mail.got(sib_ref.at[i], bsem.at[i], w.tok_dev(0, 0, 1))
            add(i * 2, slice(None), lambda r, i=i: sib_ref[i, r, :])
            if dy == 1:
                mail.send(o_ref.at[i * 2, :, P], yp_ref.at[dx], psem.at[dx], w.tok_dev(0, 1, 0))
            if dx != 0:
                b = (NX - dx - 1) * 2 + dy
                mail.send(o_ref.at[i * 2, :, Q], xq_ref.at[b], qsem.at[b], w.tok_dev(dx, 0, 0))

    def y_sum(dx):
        mail.got(yp_ref.at[dx], psem.at[dx], w.tok_dev(0, 1, 0))
        add(slot(dx, 0, 0), P, lambda r: yp_ref[dx, r, :])
        if dx != 0:
            b = NX - dx - 1
            mail.send(o_ref.at[slot(dx, 0, 0), :, P], xp_ref.at[b], fsem.at[b], w.tok_dev(dx, 0, 0))

    def x_sum(dy):
        for b in range(3):
            mail.got(xq_ref.at[b * 2 + dy], qsem.at[b * 2 + dy], w.tok_dev(1, 0, 0))
        add(slot(0, dy, 0), Q, *[lambda r, b=b: xq_ref[b * 2 + dy, r, :] for b in range(3)])
        if dy == 1:
            mail.send(o_ref.at[slot(0, 1, 0), :, Q], yq_ref, fsem.at[3], w.tok_dev(0, 1, 0))

    ag.y_in()
    ag.sib_in(0, 0)
    ag.sib_in(0, 1)
    loads[0].wait()
    loads[1].wait()
    compute(0)
    pair_out(0)
    for dx in (1, 3, 2):
        ag.x_in(dx)
    for dx in (1, 3):
        ag.x_in_late(dx)
    ag.x_in_late(2)
    ag.sib_in(1, 0)
    ag.sib_in(3, 0)
    compute(1)
    pair_out(1)
    for dx in (2, 1, 3):
        ag.far_in(dx)
    pair_in(0)
    ag.sib_in(2, 0)
    ag.sib_in(2, 1)
    compute(2)
    pair_out(2)
    pair_in(1)
    ag.sib_in(1, 1)
    ag.sib_in(3, 1)
    compute(3)
    pair_out(3)
    pair_in(2)
    y_sum(2)
    pair_in(3)
    y_sum(1)
    y_sum(3)
    x_sum(1)
    y_sum(0)
    x_sum(0)

    for b in range(3):
        mail.got(xp_ref.at[b], fsem.at[b], w.tok_dev(1, 0, 0))
    mail.got(yq_ref, fsem.at[3], w.tok_dev(0, 1, 0))

    def final(cols, srcs):
        v = o_ref[0, :, cols].astype(f32)
        for src in srcs:
            v = v + src.astype(f32)
        return lax.dot_general(
            sel, (v * gate_col).astype(bf16), (((0,), (0,)), ((), ())), preferred_element_type=f32
        ).astype(bf16)

    con_ref[:, P] = final(P, [xp_ref[b] for b in range(3)])
    con_ref[:, Q] = final(Q, [yq_ref[...]])
    for k in range(1, NE):
        mail.send(con_ref.at[of(w.exp(k))], rec_ref.at[k - 1], esem.at[k - 1], {"expert": w.exp(k)})
    total = hid_ref[...].astype(f32) + con_ref[me, :].astype(f32)
    for k in range(1, NE):
        mail.got(rec_ref.at[k - 1], esem.at[k - 1], {"expert": w.exp(k)})
        total = total + rec_ref[k - 1].astype(f32)
    out_ref[...] = total.astype(bf16)
    mail.drain()


def expert_layer(normed, route, hidden, w_router, w_expert):
    rows, model = normed.shape
    units = w_expert.shape[3]
    toks, cap = rows * NE, 80
    cut = model * 5 // 8
    vm = pl.BlockSpec(memory_space=pltpu.VMEM)
    sends = 2 * (NE - 1) + AG_SENDS + 8 + 4 + 6 + 3 + 1 + NE - 1
    dma = pltpu.SemaphoreType.DMA
    return pl.pallas_call(
        expert_kernel,
        out_shape=jax.ShapeDtypeStruct((rows, model), bf16),
        in_specs=[vm] * 4 + [pl.BlockSpec(memory_space=pl.ANY)],
        out_specs=vm,
        scratch_shapes=[
            pltpu.VMEM((3, model, units), bf16),
            pltpu.VMEM((toks, model), bf16),
            pltpu.VMEM((toks, 128), bf16),
            pltpu.VMEM((16, cap, model), bf16),
            pltpu.VMEM((4 * cap, units), bf16),
            pltpu.VMEM((16, cap, model), bf16),
            pltpu.VMEM((8, cap, model), bf16),
            pltpu.VMEM((4, cap, cut), bf16),
            pltpu.VMEM((cap, model - cut), bf16),
            pltpu.VMEM((3, cap, cut), bf16),
            pltpu.VMEM((6, cap, model - cut), bf16),
            pltpu.VMEM((toks, model), bf16),
            pltpu.VMEM((NE - 1, rows, model), bf16),
            dma((3,)), dma((sends,)), dma((NE - 1,)), dma((NE - 1,)), dma((16, 2)), dma((8,)),
            dma((4,)), dma((6,)), dma((4,)), dma((NE - 1,)),
        ],
        compiler_params=pltpu.CompilerParams(
            collective_id=2, has_side_effects=True, vmem_limit_bytes=60 * 2**20
        ),
        cost_estimate=pl.CostEstimate(
            flops=6 * 16 * cap * model * units, bytes_accessed=20 * 2**20, transcendentals=0
        ),
        name="expert_layer",
    )(normed, route, hidden, w_router, w_expert)


def on_device(
    x_in, conv_w, b_proj, c_proj, log_decay, d_skip, w_out, norm_gain, w_router, w_expert, route_ids
):
    seq_rows, chan_dev = x_in.shape
    tail_rows = x_in[seq_rows - (CONV - 1) :]
    earlier_rows = from_behind(tail_rows, "tok", 1)
    extended = jnp.concatenate([earlier_rows, x_in], axis=0).astype(jnp.float32)
    conv_sum = conv_w[0] * extended[0:seq_rows]
    for offset in range(1, CONV):
        conv_sum = conv_sum + conv_w[offset] * extended[offset : offset + seq_rows]
    conv_out = jax.nn.silu(conv_sum)
    heads_dev = chan_dev // HEAD
    blocks = seq_rows // BLOCK
    x_heads = conv_out.reshape(blocks, BLOCK, heads_dev, HEAD)
    b_blocks = b_proj.astype(jnp.float32).reshape(blocks, BLOCK, N_STATE)
    c_blocks = c_proj.astype(jnp.float32).reshape(blocks, BLOCK, N_STATE)
    decay_blocks = log_decay.reshape(blocks, BLOCK, heads_dev)

    def local_step(carry_pair, inputs):
        carry_decay, carry_state = carry_pair
        y_local, state_block, total_decay, entry_decay = block_terms(*inputs)
        advanced = (
            carry_decay * total_decay,
            total_decay[:, None, None] * carry_state + state_block,
        )
        return (advanced, (y_local, entry_decay, carry_decay, carry_state))

    identity = (
        jnp.ones((heads_dev,), jnp.float32),
        jnp.zeros((heads_dev, HEAD, N_STATE), jnp.float32),
    )
    device_total, stacked = lax.scan(
        local_step, identity, (x_heads, b_blocks, c_blocks, decay_blocks)
    )
    y_locals, entry_decays, lead_decays, lead_states = stacked
    prefix = prefix_state(*device_total, "tok")
    incoming = lead_decays[:, :, None, None] * prefix[None] + lead_states
    y_carry = jnp.einsum("bhi,bin,bhpn->bihp", entry_decays, c_blocks, incoming, precision=highest)
    mixed = (y_locals + y_carry).reshape(seq_rows, heads_dev, HEAD) + d_skip[
        None, :, None
    ] * conv_out.reshape(seq_rows, heads_dev, HEAD)
    scan_out = mixed.reshape(seq_rows, chan_dev).astype(jnp.bfloat16)
    rows, model = route_ids.shape[1], norm_gain.shape[0]
    route = jnp.pad(route_ids[0].astype(jnp.bfloat16), ((0, 0), (0, 126)))
    hidden, normed = project(scan_out, w_out, norm_gain[None], rows)
    layer_out = expert_layer(normed, route, hidden, w_router, w_expert)
    return layer_out.reshape(1, rows, model)


def solution(mesh):
    placed = (
        P("tok", "expert"),
        P(None, "expert"),
        P("tok", None),
        P("tok", None),
        P("tok", "expert"),
        P("expert"),
        P("expert", "tok"),
        P(),
        P(),
        P("expert", None, None, "tok"),
        P("tok", "expert", None),
    )
    return jax.shard_map(
        on_device, mesh=mesh, in_specs=placed, out_specs=P("tok", "expert", None), check_vma=False
    )
```

time: 430 us -> 294 us (0.68)
  waiting for transfers between devices: 286 us -> 38.4 us
  Pallas kernels: 0 us -> 215 us
  matrix products: 50.1 us -> 3.95 us
  blocking collectives: 46.1 us -> 0 us
  starting transfers between devices: 9.17 us -> 1.95 us
    pallas_call x0 -> x2, Pallas kernels: none -> 215 us  [the longest x1 148 us: expert_layer(): pl.pallas_call(expert_kernel, out_shape=jax.ShapeDtypeStruct((rows, model...]
    reduce_scatter x2 -> x0, waiting for transfers between devices: 146 us -> none  [the longest x1 73.7 us: on_device(): lax.psum_scatter(partials.astype(jnp.bfloat16), 'tok', scatter_dimension=...]
    all_gather x3 -> x1, waiting for transfers between devices: 120 us -> 37.4 us  [prefix_state(): gathered = lax.all_gather(packed, axis)]
    dot_general x8 -> x1, matrix products: 45.5 us -> 0.87 us  [block_terms(): cumulative = jnp.einsum('ij,jh->hi', ones, decay_block, precision=highest)]
    unnamed x1 -> x0, blocking collectives: 26.2 us -> none
    all_to_all x1 -> x0, blocking collectives: 19.9 us -> none  [on_device(): lax.all_to_all(outgoing.reshape(experts, hot_slots, model_width), 'expert...]
    all_to_all x1 -> x0, waiting for transfers between devices: 16.7 us -> none  [on_device(): lax.all_to_all(summed.reshape(experts, hot_slots, model_width).astype(jnp...]
    all_to_all x1 -> x0, starting transfers between devices: 6.87 us -> none  [on_device(): lax.all_to_all(summed.reshape(experts, hot_slots, model_width).astype(jnp...]
  transfers between devices with their start and end apart: 7 -> 2, of which waited for: 7 -> 2; matrix products, arithmetic and copies ran while one was open for 4% -> 2% of each run, Pallas kernels for 0% -> 0%
where the time goes in v1:
time: 294 us; the launch traced here: 290 us
  Pallas kernels  215 us (73%)
  waiting for transfers between devices  38.4 us (13%)
  between operations  13.6 us (5%)
  other arithmetic  9.85 us (3%)
  local copies, waits for them, and re-layouts  7.51 us (3%)
  matrix products  3.95 us (1%)
    pallas_call x1, Pallas kernels, expert_layer(): pl.pallas_call(expert_kernel, out_shape=jax.ShapeDtypeStruct((rows, model...  148 us
    pallas_call x1, Pallas kernels, project(): pl.pallas_call(project_kernel, out_shape=[jax.ShapeDtypeStruct((rows, mod...  66.7 us
    all_gather x1, waiting for transfers between devices, prefix_state(): gathered = lax.all_gather(packed, axis)  37.4 us
    convert_element_type x6, other arithmetic, one(): lax.dynamic_index_in_dim(gathered, step, 0, False).astype(jnp.float32)  6.03 us
  transfers between devices with their start and end apart: 2, of which 2 were waited for; matrix products, arithmetic and copies ran while one was open for 2% of the time, Pallas kernels for 0%

profile of v1, /device:TPU:6, one launch (start us, length us, event | category | flops | bytes accessed | tf_op | source)
XLA Modules:
  0.0 290.1 jit_solution(6623596949451088119)
XLA Ops:
  6.5 0.0 copy-start
  6.5 0.0 copy-start.7
  6.5 0.0 copy-start.6
  6.5 0.0 copy-start.8
  6.5 0.0 copy-start.5
  6.5 0.0 all-gather.2.cloned.1.call-start
  6.6 0.8 slice.39
  7.4 1.9 collective-permute-start
  9.3 0.9 fusion.27
  10.2 0.9 convolution_bitcast_fusion.2
  11.0 0.2 slice_reduce_fusion
  11.3 0.1 exponential_bitcast_fusion.1
  11.4 1.0 collective-permute-done
  12.3 1.0 maximum_convert_fusion
  13.3 0.3 divide_multiply_fusion
  13.7 0.2 copy.21
  13.9 0.0 copy-done
  13.9 0.4 fusion.3
  14.3 0.1 broadcast_in_dim.72
  14.3 0.8 pad_maximum_fusion
  15.1 0.0 all-gather.2.cloned.1.call-update
  15.1 0.0 copy-done.7
  15.1 0.1 mul.116
  15.2 0.1 mul.117
  15.3 0.0 copy-done.6
  15.3 1.3 copy.24.wr_ref
  16.6 0.0 copy-done.8
  16.6 0.1 copy.23
  16.7 0.6 pad.4.rt_ref
  17.4 0.0 copy-done.5
  17.4 0.1 fusion.28
  17.5 37.4 %all-gather.2.cloned.1.call-done = bf16[16,16,72,128]{3,2,1,0:T(8,128)(2,1)} async-done(((bf16[1,16,72,128]{3,2,1,0:T(8,128)(2,1)}), bf16[16,16,72,128]{3,2,1,0:T(8,128)(2,1)}) %all-gather.2.cloned.1.call-update) | async-done | bytes 4718608 | tf_op jit(solution)/shard_map/all_gather | solution.py:28
  55.0 7.6 %while.2 = (s32[]{:T(128)}, f32[16,64,128]{2,1,0:T(8,128)S(1)}, s32[]{:T(128)}, bf16[16,16,72,128]{3,2,1,0:T(8,128)(2,1)}, s32[]{:T(128)}, /*index=5*/s32[]{:T(128)}, s32[]{:T(128)}) while((s32[]{:T(128)}, f32[16,64,128]{2,1,0:T(8,128)S(1)}, s32[]{:T(128)}, bf16[16,16,72,128]{3,2,1,0:T(8,128)(2,1)}, s32[]{:T(128)}, /*index=5*/s32[]{:T(128)}, ...), condition=%wide.region_1.2_spmd, body=%wide.region_0.1_spmd.sunk | while | flops 409605 | bytes 2482291 | solution.py:35
  55.0 1.0 bitcast_convert_fusion.2
  56.0 0.2 slice_add_fusion.2
  56.2 1.0 bitcast_convert_fusion.2
  57.3 0.2 slice_add_fusion.2
  57.5 1.0 bitcast_convert_fusion.2
  58.5 0.2 slice_add_fusion.2
  58.8 1.0 bitcast_convert_fusion.2
  59.8 0.2 slice_add_fusion.2
  60.0 1.0 bitcast_convert_fusion.2
  61.0 0.2 slice_add_fusion.2
  61.3 1.0 bitcast_convert_fusion.2
  62.3 0.2 slice_add_fusion.2
  62.5 0.0 copy-start.1
  62.5 0.0 copy-start.2
  62.6 0.4 fusion.1
  62.9 2.2 fusion
  65.1 0.2 copy.22
  65.3 0.4 add_convert_fusion.scan_ref
  65.7 0.0 copy-done.1
  65.7 0.0 copy-done.2
  65.7 66.7 %project.1 = (bf16[16,4096]{1,0:T(8,128)(2,1)S(1)}, bf16[16,4096]{1,0:T(8,128)(2,1)S(1)}) custom-call(bf16[128,1024]{1,0:T(8,128)(2,1)S(1)} %add_convert_fusion.scan_ref, bf16[1024,256]{1,0:T(8,128)(2,1)S(1)} %copy-done.1, f32[1,4096]{1,0:T(1,128)S(1)} %bitcast.45), custom_call_target="tpu_custom_call" | custom-call | flops 1073741824 | bytes 20971520 | tf_op jit(solution)/shard_map/project/pallas_call | solution.py:253
  132.4 0.0 copy-start.3
  132.5 0.6 copy-done.3
  133.1 0.0 copy-start.4
  133.1 0.7 copy-done.4
  133.8 148.0 %expert_layer.1 = bf16[16,4096]{1,0:T(8,128)(2,1)} custom-call(bf16[16,4096]{1,0:T(8,128)(2,1)} %copy-done.4, bf16[16,128]{1,0:T(8,128)(2,1)} %pad.4.rt_ref, bf16[16,4096]{1,0:T(8,128)(2,1)} %copy-done.3, bf16[4096,8]{1,0:T(8,128)(2,1)} %copy.24.wr_ref, bf16[1,3,4096,768]{3,2,1,0:T(8,128)(2,1)} %we_ref.1), custom_call_target="tpu_custom_call" | custom-call | flops 24159191040 | bytes 20971520 | tf_op jit(solution)/shard_map/expert_layer/pallas_call | solution.py:471
  281.7 1.6 copy.32
  (10 shorter events, 0.1 us)
Async XLA Ops:
  6.5 7.3 %copy-start = (bf16[128,128]{1,0:T(8,128)(2,1)S(1)}, bf16[128,128]{1,0:T(8,128)(2,1)}, u32[]{:S(2)}) copy-start(bf16[128,128]{1,0:T(8,128)(2,1)} %param.15) | copy-start | bytes 98308
  6.5 8.6 %copy-start.7 = (f32[16]{0:T(128)S(1)}, f32[16]{0:T(128)}, u32[]{:S(2)}) copy-start(f32[16]{0:T(128)} %param.18) | copy-start | bytes 196
  6.5 8.7 %copy-start.6 = (bf16[4096,8]{0,1:T(8,128)(2,1)S(1)}, bf16[4096,8]{0,1:T(8,128)(2,1)}, u32[]{:S(2)}) copy-start(bf16[4096,8]{0,1:T(8,128)(2,1)} %param.21) | copy-start | bytes 196612
  6.5 10.1 %copy-start.8 = (s32[1,16,2]{1,2,0:T(2,128)S(1)}, s32[1,16,2]{1,2,0:T(2,128)}, u32[]{:S(2)}) copy-start(s32[1,16,2]{1,2,0:T(2,128)} %param.23) | copy-start | bytes 388
  6.5 10.8 %copy-start.5 = (bf16[128,128]{1,0:T(8,128)(2,1)S(1)}, bf16[128,128]{1,0:T(8,128)(2,1)}, u32[]{:S(2)}) copy-start(bf16[128,128]{1,0:T(8,128)(2,1)} %param.16) | copy-start | bytes 98308
  6.5 48.4 %all-gather.2.cloned.1.call-start = ((), (), s32[]{:S(2)}) async-start(), calls=%async_computation | async-start | bytes 5013504 | tf_op jit(solution)/shard_map/all_gather | solution.py:28
  7.4 5.0 %collective-permute-start = (bf16[3,1024]{1,0:T(4,128)(2,1)S(1)}, bf16[3,1024]{1,0:T(4,128)(2,1)S(1)}, u32[]{:S(2)}, u32[]{:S(2)}) collective-permute-start(bf16[3,1024]{1,0:T(4,128)(2,1)S(1)} %slice.39), channel_id=1, source_target_pairs={{0,1},{1,2},{2,3},{3,4},{4,5},{5,6},{6,7},{7,8},{8,9},{9,10},{10,1... | collective-permute-start | bytes 18440 | tf_op jit(solution)/shard_map/ppermute | solution.py:20
  62.5 3.2 %copy-start.1 = (bf16[1024,256]{1,0:T(8,128)(2,1)S(1)}, bf16[1024,256]{1,0:T(8,128)(2,1)}, u32[]{:S(2)}) copy-start(bf16[1024,256]{1,0:T(8,128)(2,1)} %wout_ref.1) | copy-start | bytes 1572868
  62.5 3.2 %copy-start.2 = (f32[4096]{0:T(1024)S(1)}, f32[4096]{0:T(1024)}, u32[]{:S(2)}) copy-start(f32[4096]{0:T(1024)} %param.20) | copy-start | bytes 49156
  132.4 0.7 copy-start.3
  133.1 0.7 copy-start.4
Sparse Core Ops, SparseCore 0:
  15.2 39.6 all-gather.1

commit v2 on v1

--- a/solution.py
+++ b/solution.py
@@ -5,56 +5,9 @@
 from jax.experimental.pallas import tpu as pltpu
 from jax.sharding import PartitionSpec as P
 
-N_STATE = 128
 CONV = 4
 HEAD = 64
-BLOCK = 128
-
-
 highest = lax.Precision.HIGHEST
-
-
-def from_behind(value, axis, steps):
-    count = lax.axis_size(axis)
-    first, last = (max(0, -steps), min(count, count - steps))
-    return lax.ppermute(value, axis, [(source, source + steps) for source in range(first, last)])
-
-
-def prefix_state(decay, state, axis):
-    heads, head, n = state.shape
-    packed = jnp.concatenate(
-        [state, jnp.broadcast_to(decay[:, None, None], (heads, 8, n))], axis=1
-    ).astype(jnp.bfloat16)
-    gathered = lax.all_gather(packed, axis)
-    place = lax.axis_index(axis)
-
-    def one(step, held):
-        item = lax.dynamic_index_in_dim(gathered, step, 0, False).astype(jnp.float32)
-        return item[:, head : head + 1] * held + item[:, :head]
-
-    return lax.fori_loop(0, place, one, jnp.zeros_like(state))
-
-
-def block_terms(x_block, b_block, c_block, decay_block):
-    length = decay_block.shape[0]
-    ones = jnp.tril(jnp.ones((length, length), jnp.float32))
-    cumulative = jnp.einsum("ij,jh->hi", ones, decay_block, precision=highest)
-    spread = cumulative[:, :, None] - cumulative[:, None, :]
-    lower_mask = (
-        jnp.arange(length, dtype=jnp.int32)[:, None] >= jnp.arange(length, dtype=jnp.int32)[None, :]
-    )
-    decay_matrix = jnp.where(
-        lower_mask[None], jnp.exp(jnp.where(lower_mask[None], spread, 0.0)), 0.0
-    )
-    scores = jnp.einsum("in,jn->ij", c_block, b_block, precision=highest)
-    y_local = jnp.einsum("hij,jhp->ihp", decay_matrix * scores[None], x_block, precision=highest)
-    tail_decay = jnp.exp(cumulative[:, -1:] - cumulative)
-    state_block = jnp.einsum("hj,jhp,jn->hpn", tail_decay, x_block, b_block, precision=highest)
-    total_decay = jnp.exp(cumulative[:, -1])
-    entry_decay = jnp.exp(cumulative)
-    return (y_local, state_block, total_decay, entry_decay)
-
-
 MESH = pl.DeviceIdType.MESH
 bf16, f32 = jnp.bfloat16, jnp.float32
 NX, NE = 4, 8
@@ -89,13 +42,16 @@
 NEAR = [(0, 0, 1), (0, 1, 0), (1, 0, 0), (3, 0, 0), (2, 0, 0)]
 
 
-def greet(w):
+def greet(w, behind=False):
     barrier = pltpu.get_barrier_semaphore()
     for d in NEAR:
         pl.semaphore_signal(barrier, inc=1, device_id=w.tok_dev(*d), device_id_type=MESH)
     for k in range(1, NE):
         pl.semaphore_signal(barrier, inc=1, device_id={"expert": w.exp(k)}, device_id_type=MESH)
-    pl.semaphore_wait(barrier, len(NEAR) + NE - 1)
+    if behind:
+        back = lax.rem(w.t + 4 * NX - 1, 4 * NX)
+        pl.semaphore_signal(barrier, inc=1, device_id={"tok": back}, device_id_type=MESH)
+    pl.semaphore_wait(barrier, len(NEAR) + NE - 1 + behind)
 
 
 class Mail:
@@ -185,14 +141,26 @@
     return hid * lax.rsqrt(ms + 1e-05) * gain
 
 
-def project_kernel(
-    scan_ref, wout_ref, gain_ref, hid_ref, nrm_ref, g_ref, part_ref, rec_ref, ssem, rsem, esem
+def mixer_kernel(
+    x_ref, cw_ref, b_ref, c_ref, ld_ref, ds_ref, wout_ref, gain_ref,
+    hid_ref, nrm_ref,
+    g_ref, part_ref, rec_ref, ext_ref, tail_ref, conv_ref, y_ref, ent_ref, st_ref, s1_ref, s2_ref,
+    r_in_ref, r_out_ref, sin_ref, hand_ref, scan_ref,
+    ssem, rsem, esem, tsem, usem,
 ):
     w = Where()
     mail = Mail(ssem)
-    depth = wout_ref.shape[0]
+    toks, chans = x_ref.shape
+    heads = ld_ref.shape[1]
+    half = chans // 2
+    n_state = b_ref.shape[1]
+    depth, width = wout_ref.shape
     cut = depth * 5 // 8
-    greet(w)
+    sib = w.tok_dev(0, 0, 1)
+    greet(w, behind=True)
+    mail.send(
+        x_ref.at[pl.ds(toks - 16, 16)], tail_ref, tsem.at[0], {"tok": lax.rem(w.t + 1, 4 * NX)}
+    )
 
     def view(s, part):
         return g_ref.at[s, pl.ds(0, cut)] if part == 0 else g_ref.at[s, pl.ds(cut, depth - cut)]
@@ -200,7 +168,151 @@
     g_ref[0] = wout_ref[...]
     ag = Gather(w, mail, view, rsem)
     ag.start()
-    width = wout_ref.shape[1]
+
+    ext_ref[16:, :] = x_ref[...].astype(f32)
+    mail.got(tail_ref, tsem.at[0], sib)
+    ext_ref[0:16, :] = jnp.where(w.t > 0, tail_ref[...].astype(f32), 0.0)
+    for b in range(chans // 256):
+        cols = pl.ds(b * 256, 256)
+        v = cw_ref[0:1, cols] * ext_ref[13 : 13 + toks, cols]
+        for k in range(1, CONV):
+            v = v + cw_ref[k : k + 1, cols] * ext_ref[13 + k : 13 + k + toks, cols]
+        conv_ref[:, cols] = v / (1.0 + jnp.exp(-v))
+
+    ii = lax.broadcasted_iota(jnp.int32, (toks, toks), 0)
+    jj = lax.broadcasted_iota(jnp.int32, (toks, toks), 1)
+    low = ii >= jj
+    lowf = jnp.where(low, 1.0, 0.0)
+    cum = jnp.dot(lowf, ld_ref[...], precision=highest, preferred_element_type=f32)
+    cum_t = lax.dot_general(
+        ld_ref[...], jnp.where(ii <= jj, 1.0, 0.0), (((0,), (0,)), ((), ())),
+        precision=highest, preferred_element_type=f32,
+    )
+    eh = lax.broadcasted_iota(jnp.int32, (heads, chans), 0) * HEAD
+    ec = lax.broadcasted_iota(jnp.int32, (heads, chans), 1)
+    spread = jnp.where((ec >= eh) & (ec < eh + HEAD), 1.0, 0.0)
+    both = jnp.concatenate([cum, cum[toks - 1 : toks] - cum], axis=0)
+    skip = jnp.dot(ds_ref[...], spread, precision=highest, preferred_element_type=f32)
+    for h in range(2):
+        for b in range(2):
+            cols = pl.ds(h * half + b * (half // 2), half // 2)
+            here = pl.ds(b * (half // 2), half // 2)
+            sp = spread[:, h * half + b * (half // 2) : h * half + (b + 1) * (half // 2)]
+            lev = jnp.exp(jnp.dot(both, sp, precision=highest, preferred_element_type=f32))
+            ent_ref[:, cols] = lev[:toks]
+            total = lev[toks - 1 : toks]
+            xw = (conv_ref[:, cols] * lev[toks:]).astype(bf16)
+            st_ref[h, 0:n_state, here] = lax.dot_general(
+                b_ref[...], xw, (((0,), (0,)), ((), ())), preferred_element_type=f32
+            ).astype(bf16)
+            hi = total.astype(bf16).astype(f32)
+            row = lax.broadcasted_iota(jnp.int32, (16, half // 2), 0)
+            st_ref[h, n_state : n_state + 16, here] = jnp.where(row == 0, hi, total - hi).astype(bf16)
+
+    mail.send(st_ref.at[1 - w.c], s1_ref, usem.at[0], sib)
+
+    scores = lax.dot_general(
+        c_ref[...], b_ref[...], (((1,), (1,)), ((), ())), preferred_element_type=f32
+    )
+    scores = jnp.where(low, scores, 0.0)
+    lane = lax.broadcasted_iota(jnp.int32, (toks, 2 * HEAD), 1)
+
+    def inside(p):
+        cols = pl.ds(p * 2 * HEAD, 2 * HEAD)
+        xc = conv_ref[:, cols]
+        mats = []
+        for h in (2 * p, 2 * p + 1):
+            gap = jnp.where(low, cum[:, h : h + 1] - cum_t[h : h + 1, :], 0.0)
+            mats.append((jnp.exp(gap) * scores).astype(bf16))
+        yy = jnp.dot(jnp.concatenate(mats, axis=0), xc.astype(bf16), preferred_element_type=f32)
+        y_ref[:, cols] = (
+            jnp.where(lane < HEAD, yy[:toks], yy[toks:])
+            + skip[:, p * 2 * HEAD : (p + 1) * 2 * HEAD] * xc
+        )
+
+    for p in range(2):
+        inside(p)
+
+    def by_rows(body):
+        @pl.loop(0, n_state // 16)
+        def _(i):
+            body(pl.ds(pl.multiple_of(i * 16, 16), 16))
+
+    def decay_of(block):
+        v = block.astype(f32)
+        return v[0:1] + v[1:2]
+
+    DEC = pl.ds(n_state, 16)
+    mail.got(s1_ref, usem.at[0], sib)
+    own_d = decay_of(st_ref[w.c, DEC, :])
+    sib_d = decay_of(s1_ref[DEC, :])
+    first = w.c == 0
+    d0 = jnp.where(first, own_d, sib_d)
+    d1 = jnp.where(first, sib_d, own_d)
+    chip_d = d0 * d1
+    chip_hi = chip_d.astype(bf16).astype(f32)
+    row = lax.broadcasted_iota(jnp.int32, (16, half), 0)
+    s2_ref[w.x, DEC, :] = jnp.where(row == 0, chip_hi, chip_d - chip_hi).astype(bf16)
+
+    def join(r):
+        own, other = st_ref[w.c, r, :].astype(f32), s1_ref[r, :].astype(f32)
+        s2_ref[w.x, r, :] = (
+            d1 * jnp.where(first, own, other) + jnp.where(first, other, own)
+        ).astype(bf16)
+
+    by_rows(join)
+    for i, dx in enumerate((1, 3, 2)):
+        mail.send(s2_ref.at[w.x], s2_ref.at[w.x], tsem.at[1 + NX - dx], w.tok_dev(dx, 0, 0))
+    for p in range(2, 5):
+        inside(p)
+    ag.y_in()
+    for p in range(5, heads // 2):
+        inside(p)
+    for dx in (1, 3, 2):
+        mail.got(s2_ref.at[lax.rem(w.x + dx, NX)], tsem.at[1 + dx], w.tok_dev(dx, 0, 0))
+    decs = [decay_of(s2_ref[k, DEC, :]) for k in range(NX)]
+    before_d = jnp.ones_like(chip_d)
+    for k in range(NX):
+        before_d = before_d * jnp.where(w.x > k, decs[k], 1.0)
+
+    def row_scan(r):
+        run = jnp.zeros((16, half), f32)
+        before = run
+        for k in range(NX):
+            before = jnp.where(w.x == k, run, before)
+            run = decs[k] * run + s2_ref[k, r, :].astype(f32)
+        r_out_ref[0, r, :] = run.astype(bf16)
+        r_out_ref[1, r, :] = before.astype(bf16)
+
+    by_rows(row_scan)
+    mail.send(r_out_ref.at[0], r_in_ref, usem.at[1], w.tok_dev(0, 1, 0))
+    for dx in (1, 3, 2):
+        ag.x_in(dx)
+    mail.got(r_in_ref, usem.at[1], w.tok_dev(0, 1, 0))
+    lower = w.y > 0
+
+    def enter(r):
+        chip = r_out_ref[1, r, :].astype(f32) + jnp.where(
+            lower, before_d * r_in_ref[r, :].astype(f32), 0.0
+        )
+        s0 = jnp.where(first, st_ref[w.c, r, :], s1_ref[r, :]).astype(f32)
+        second = d0 * chip + s0
+        sin_ref[w.c, r, :] = jnp.where(first, chip, second).astype(bf16)
+        hand_ref[r, :] = jnp.where(first, second, chip).astype(bf16)
+
+    by_rows(enter)
+    mail.send(hand_ref, sin_ref.at[w.c], usem.at[2], sib)
+
+    def close(h):
+        for b in range(2):
+            cols = pl.ds(pl.multiple_of(h * half + b * (half // 2), half // 2), half // 2)
+            here = pl.ds(b * (half // 2), half // 2)
+            carry = jnp.dot(c_ref[...], sin_ref[h, :, here], preferred_element_type=f32)
+            scan_ref[:, cols] = (y_ref[:, cols] + ent_ref[:, cols] * carry).astype(bf16)
+
+    close(w.c)
+    mail.got(sin_ref.at[1 - w.c], usem.at[2], sib)
+    close(1 - w.c)
 
     def mult(dx, dy, dc):
         cols = pl.ds(pl.multiple_of(w.tok(dx, dy, dc) * width, width), width)
@@ -208,25 +320,24 @@
             scan_ref[...], g_ref[slot(dx, dy, dc)], preferred_element_type=f32
         ).astype(bf16)
 
+    for dx in (1, 3, 2):
+        ag.x_in_late(dx)
     mult(0, 0, 0)
-    ag.y_in()
-    for dx in (1, 3, 2):
-        ag.x_in(dx)
     ag.sib_in(0, 0)
     mult(0, 0, 1)
     mult(0, 1, 0)
-    for dx in (1, 3, 2):
-        ag.x_in_late(dx)
-        mult(dx, 0, 0)
     ag.sib_in(0, 1)
     mult(0, 1, 1)
     for dx in (1, 3, 2):
+        mult(dx, 0, 0)
+        ag.sib_in(dx, 0)
+        mult(dx, 0, 1)
+    for dx in (1, 3, 2):
         ag.far_in(dx)
         mult(dx, 1, 0)
-    for dy in (0, 1):
-        for dx in (1, 3, 2):
-            ag.sib_in(dx, dy)
-            mult(dx, dy, 1)
+    for dx in (1, 3, 2):
+        ag.sib_in(dx, 1)
+        mult(dx, 1, 1)
     rows = hid_ref.shape[0]
 
     def mine(e):
@@ -246,22 +357,40 @@
     mail.drain()
 
 
-def project(scan_out, w_out, gain, rows):
+def mixer(x_in, conv_w, b_proj, c_proj, log_decay, d_skip, w_out, gain, rows):
     depth, width = w_out.shape
-    toks, model = scan_out.shape[0], gain.shape[1]
+    toks, chans = x_in.shape
+    model, n_state = gain.shape[1], b_proj.shape[1]
+    half = chans // 2
     vm = pl.BlockSpec(memory_space=pltpu.VMEM)
+    dma = pltpu.SemaphoreType.DMA
     return pl.pallas_call(
-        project_kernel,
+        mixer_kernel,
         out_shape=[jax.ShapeDtypeStruct((rows, model), bf16)] * 2,
-        in_specs=[vm] * 3,
+        in_specs=[vm] * 8,
         out_specs=[vm] * 2,
         scratch_shapes=[
             pltpu.VMEM((16, depth, width), bf16),
             pltpu.VMEM((toks, model), bf16),
             pltpu.VMEM((NE - 1, rows, model), bf16),
-            pltpu.SemaphoreType.DMA((AG_SENDS + NE - 1,)),
-            pltpu.SemaphoreType.DMA((16, 2)),
-            pltpu.SemaphoreType.DMA((NE - 1,)),
+            pltpu.VMEM((toks + 16, chans), f32),
+            pltpu.VMEM((16, chans), bf16),
+            pltpu.VMEM((toks, chans), f32),
+            pltpu.VMEM((toks, chans), f32),
+            pltpu.VMEM((toks, chans), f32),
+            pltpu.VMEM((2, n_state + 16, half), bf16),
+            pltpu.VMEM((n_state + 16, half), bf16),
+            pltpu.VMEM((NX, n_state + 16, half), bf16),
+            pltpu.VMEM((n_state, half), bf16),
+            pltpu.VMEM((2, n_state, half), bf16),
+            pltpu.VMEM((2, n_state, half), bf16),
+            pltpu.VMEM((n_state, half), bf16),
+            pltpu.VMEM((toks, chans), bf16),
+            dma((AG_SENDS + NE - 1 + 7,)),
+            dma((16, 2)),
+            dma((NE - 1,)),
+            dma((1 + NX,)),
+            dma((3,)),
         ],
         compiler_params=pltpu.CompilerParams(
             collective_id=1, has_side_effects=True, vmem_limit_bytes=40 * 2**20
@@ -269,8 +398,8 @@
         cost_estimate=pl.CostEstimate(
             flops=2 * toks * depth * model, bytes_accessed=20 * 2**20, transcendentals=0
         ),
-        name="project",
-    )(scan_out, w_out, gain)
+        name="mixer",
+    )(x_in, conv_w, b_proj, c_proj, log_decay, d_skip, w_out, gain)
 
 
 def expert_kernel(
@@ -503,48 +632,11 @@
 def on_device(
     x_in, conv_w, b_proj, c_proj, log_decay, d_skip, w_out, norm_gain, w_router, w_expert, route_ids
 ):
-    seq_rows, chan_dev = x_in.shape
-    tail_rows = x_in[seq_rows - (CONV - 1) :]
-    earlier_rows = from_behind(tail_rows, "tok", 1)
-    extended = jnp.concatenate([earlier_rows, x_in], axis=0).astype(jnp.float32)
-    conv_sum = conv_w[0] * extended[0:seq_rows]
-    for offset in range(1, CONV):
-        conv_sum = conv_sum + conv_w[offset] * extended[offset : offset + seq_rows]
-    conv_out = jax.nn.silu(conv_sum)
-    heads_dev = chan_dev // HEAD
-    blocks = seq_rows // BLOCK
-    x_heads = conv_out.reshape(blocks, BLOCK, heads_dev, HEAD)
-    b_blocks = b_proj.astype(jnp.float32).reshape(blocks, BLOCK, N_STATE)
-    c_blocks = c_proj.astype(jnp.float32).reshape(blocks, BLOCK, N_STATE)
-    decay_blocks = log_decay.reshape(blocks, BLOCK, heads_dev)
-
-    def local_step(carry_pair, inputs):
-        carry_decay, carry_state = carry_pair
-        y_local, state_block, total_decay, entry_decay = block_terms(*inputs)
-        advanced = (
-            carry_decay * total_decay,
-            total_decay[:, None, None] * carry_state + state_block,
-        )
-        return (advanced, (y_local, entry_decay, carry_decay, carry_state))
-
-    identity = (
-        jnp.ones((heads_dev,), jnp.float32),
-        jnp.zeros((heads_dev, HEAD, N_STATE), jnp.float32),
+    rows, model = route_ids.shape[1], norm_gain.shape[0]
+    route = jnp.pad(route_ids[0].astype(bf16), ((0, 0), (0, 126)))
+    hidden, normed = mixer(
+        x_in, conv_w, b_proj, c_proj, log_decay, d_skip[None], w_out, norm_gain[None], rows
     )
-    device_total, stacked = lax.scan(
-        local_step, identity, (x_heads, b_blocks, c_blocks, decay_blocks)
-    )
-    y_locals, entry_decays, lead_decays, lead_states = stacked
-    prefix = prefix_state(*device_total, "tok")
-    incoming = lead_decays[:, :, None, None] * prefix[None] + lead_states
-    y_carry = jnp.einsum("bhi,bin,bhpn->bihp", entry_decays, c_blocks, incoming, precision=highest)
-    mixed = (y_locals + y_carry).reshape(seq_rows, heads_dev, HEAD) + d_skip[
-        None, :, None
-    ] * conv_out.reshape(seq_rows, heads_dev, HEAD)
-    scan_out = mixed.reshape(seq_rows, chan_dev).astype(jnp.bfloat16)
-    rows, model = route_ids.shape[1], norm_gain.shape[0]
-    route = jnp.pad(route_ids[0].astype(jnp.bfloat16), ((0, 0), (0, 126)))
-    hidden, normed = project(scan_out, w_out, norm_gain[None], rows)
     layer_out = expert_layer(normed, route, hidden, w_router, w_expert)
     return layer_out.reshape(1, rows, model)
 

time: 294 us -> 246 us (0.84)
  waiting for transfers between devices: 38.4 us -> 0 us
  Pallas kernels: 215 us -> 232 us
  between operations: 13.6 us -> 0.04 us
  other arithmetic: 9.85 us -> 0.68 us
  local copies, waits for them, and re-layouts: 7.51 us -> 12.1 us
  matrix products: 3.95 us -> 0 us
    all_gather x1 -> x0, waiting for transfers between devices: 37.4 us -> none  [prefix_state(): gathered = lax.all_gather(packed, axis)]
    pallas_call x1, Pallas kernels: 66.7 us -> 78.8 us  [mixer(): pl.pallas_call(mixer_kernel, out_shape=[jax.ShapeDtypeStruct((rows, model...]
    unnamed x20 -> x21, local copies, waits for them, and re-layouts: 4.25 us -> 11.4 us
    convert_element_type x9 -> x1, other arithmetic: 7.42 us -> 0.68 us  [on_device(): route = jnp.pad(route_ids[0].astype(bf16), ((0, 0), (0, 126)))]
    pallas_call x1, Pallas kernels: 148 us -> 153 us  [expert_layer(): pl.pallas_call(expert_kernel, out_shape=jax.ShapeDtypeStruct((rows, model...]
    dot_general x5 -> x0, matrix products: 3.95 us -> none  [the longest x1 2.19 us: block_terms(): jnp.einsum('hij,jhp->ihp', decay_matrix * scores[None], x_block, precisio...]
  transfers between devices with their start and end apart: 2 -> 0, of which waited for: 2 -> 0; matrix products, arithmetic and copies ran while one was open for 2% -> 0% of each run, Pallas kernels for 0% -> 0%
where the time goes in v2:
time: 246 us; the launch traced here: 245 us
  Pallas kernels  232 us (94%)
  local copies, waits for them, and re-layouts  12.1 us (5%)
    pallas_call x1, Pallas kernels, expert_layer(): pl.pallas_call(expert_kernel, out_shape=jax.ShapeDtypeStruct((rows, model...  153 us
    pallas_call x1, Pallas kernels, mixer(): pl.pallas_call(mixer_kernel, out_shape=[jax.ShapeDtypeStruct((rows, model...  78.8 us
    unnamed x21, local copies, waits for them, and re-layouts  11.4 us

profile of v2, /device:TPU:6, one launch (start us, length us, event | category | flops | bytes accessed | tf_op | source)
XLA Modules:
  0.0 244.7 jit_solution(9893214277193542213)
XLA Ops:
  0.0 0.7 convert_bitcast_fusion
  0.7 0.1 copy.13
  0.8 0.6 pad.4.rt_ref
  1.4 0.8 copy.12.ld_ref
  2.2 0.0 copy-start
  2.2 1.0 copy-done
  3.2 0.0 copy-start.1
  3.2 0.9 copy-done.1
  4.2 0.0 copy-start.2
  4.2 0.8 copy-done.2
  4.9 0.0 copy-start.3
  4.9 0.8 copy-done.3
  5.7 0.0 copy-start.4
  5.7 0.7 copy-done.4
  6.4 0.0 copy-start.5
  6.4 0.7 copy-done.5
  7.1 0.0 copy-start.6
  7.1 0.7 copy-done.6
  7.8 78.8 %mixer.1 = (bf16[16,4096]{1,0:T(8,128)(2,1)S(1)}, bf16[16,4096]{1,0:T(8,128)(2,1)S(1)}) custom-call(bf16[128,1024]{1,0:T(8,128)(2,1)S(1)} %copy-done.1, f32[4,1024]{1,0:T(4,128)S(1)} %copy-done.4, bf16[128,128]{1,0:T(8,128)(2,1)S(1)} %copy-done.2, bf16[128,128]{1,0:T(8,128)(2,1)S(1)} %copy-done.3, f32[128,16]{1,0:T(8,128)S(1)} %copy.12.ld_ref, ...), custom_call_target="tpu_custom_call" | custom-call | flops 1073741824 | bytes 20971520 | tf_op jit(solution)/shard_map/mixer/pallas_call | solution.py:367
  86.6 0.0 copy-start.7
  86.6 0.6 copy-done.7
  87.3 0.0 copy-start.8
  87.3 0.7 copy-done.8
  87.9 2.1 copy.14.wr_ref
  90.1 153.1 %expert_layer.1 = bf16[16,4096]{1,0:T(8,128)(2,1)} custom-call(bf16[16,4096]{1,0:T(8,128)(2,1)} %copy-done.8, bf16[16,128]{1,0:T(8,128)(2,1)} %pad.4.rt_ref, bf16[16,4096]{1,0:T(8,128)(2,1)} %copy-done.7, bf16[4096,8]{1,0:T(8,128)(2,1)} %copy.14.wr_ref, bf16[1,3,4096,768]{3,2,1,0:T(8,128)(2,1)} %we_ref.1), custom_call_target="tpu_custom_call" | custom-call | flops 24159191040 | bytes 20971520 | tf_op jit(solution)/shard_map/expert_layer/pallas_call | solution.py:600
  243.2 1.6 copy.16
Async XLA Ops:
  2.2 1.0 copy-start
  3.2 0.9 copy-start.1
  4.2 0.8 copy-start.2
  4.9 0.8 copy-start.3
  5.7 0.7 copy-start.4
  6.4 0.7 copy-start.5
  7.1 0.7 copy-start.6
  86.6 0.7 copy-start.7
  87.3 0.7 copy-start.8

commit v3 on v2

--- a/solution.py
+++ b/solution.py
@@ -11,7 +11,7 @@
 MESH = pl.DeviceIdType.MESH
 bf16, f32 = jnp.bfloat16, jnp.float32
 NX, NE = 4, 8
-ORDER = [(0, 0), (0, 1), (1, 0), (3, 0), (2, 0), (2, 1), (1, 1), (3, 1)]
+ORDER = [(0, 0), (0, 1), (1, 0), (3, 0), (2, 0), (1, 1), (3, 1), (2, 1)]
 PLACE = {d: i for i, d in enumerate(ORDER)}
 
 
@@ -92,27 +92,27 @@
         s = slot(dx, dy, dc)
         self.mail.got(self.view(s, part), self.rsems.at[s, part], self.w.tok_dev(0, 0, 1))
 
-    def start(self):
-        own = (0, 0, 0)
-        for part in (1, 0):
-            self.put(own, part, (0, 1, 0), (0, 1, 0))
+    def start(self, part):
+        self.own_y(part)
+        self.own_x(part)
+        self.put((0, 0, 0), part, (0, 0, 1), (0, 0, 1))
+
+    def own_y(self, part):
+        self.put((0, 0, 0), part, (0, 1, 0), (0, 1, 0))
+
+    def own_x(self, part):
         for dx in (1, 3, 2):
-            self.put(own, 0, (dx, 0, 0), (-dx, 0, 0))
-        for dx in (1, 3, 2):
-            self.put(own, 1, (dx, 0, 0), (-dx, 0, 0))
-        for part in (0, 1):
-            self.put(own, part, (0, 0, 1), (0, 0, 1))
+            self.put((0, 0, 0), part, (dx, 0, 0), (-dx, 0, 0))
 
     def sib(self, dx, dy, part):
         self.put((dx, dy, 0), part, (0, 0, 1), (dx, dy, 1))
 
-    def y_in(self):
-        self.got(0, 1, 0, 1)
-        for dx in (1, 3, 2):
-            self.put((0, 1, 0), 1, (dx, 0, 0), (-dx, 1, 0))
-        self.sib(0, 1, 1)
-        self.got(0, 1, 0, 0)
-        self.sib(0, 1, 0)
+    def y_in(self, part):
+        self.got(0, 1, 0, part)
+        if part == 1:
+            for dx in (1, 3, 2):
+                self.put((0, 1, 0), 1, (dx, 0, 0), (-dx, 1, 0))
+        self.sib(0, 1, part)
 
     def x_in(self, dx):
         self.got(dx, 0, 0, 0)
@@ -142,22 +142,33 @@
 
 
 def mixer_kernel(
-    x_ref, cw_ref, b_ref, c_ref, ld_ref, ds_ref, wout_ref, gain_ref,
+    x_hbm, cw_hbm, b_hbm, c_hbm, ld_hbm, ds_hbm, wout_ref, gain_hbm,
     hid_ref, nrm_ref,
+    x_ref, cw_ref, b_ref, c_ref, ld_ref, ds_ref, gain_ref,
     g_ref, part_ref, rec_ref, ext_ref, tail_ref, conv_ref, y_ref, ent_ref, st_ref, s1_ref, s2_ref,
     r_in_ref, r_out_ref, sin_ref, hand_ref, scan_ref,
-    ssem, rsem, esem, tsem, usem,
+    ssem, rsem, esem, tsem, usem, lsem,
 ):
     w = Where()
     mail = Mail(ssem)
+    loads = [
+        pltpu.make_async_copy(src, dst, lsem.at[i])
+        for i, (src, dst) in enumerate((
+            (x_hbm, x_ref), (wout_ref, g_ref.at[0]), (cw_hbm, cw_ref), (ld_hbm, ld_ref),
+            (b_hbm, b_ref), (c_hbm, c_ref), (ds_hbm, ds_ref), (gain_hbm, gain_ref),
+        ))
+    ]
+    for cp in loads:
+        cp.start()
     toks, chans = x_ref.shape
-    heads = ld_ref.shape[1]
+    heads = ld_ref.shape[0]
     half = chans // 2
     n_state = b_ref.shape[1]
     depth, width = wout_ref.shape
     cut = depth * 5 // 8
     sib = w.tok_dev(0, 0, 1)
     greet(w, behind=True)
+    loads[0].wait()
     mail.send(
         x_ref.at[pl.ds(toks - 16, 16)], tail_ref, tsem.at[0], {"tok": lax.rem(w.t + 1, 4 * NX)}
     )
@@ -165,9 +176,13 @@
     def view(s, part):
         return g_ref.at[s, pl.ds(0, cut)] if part == 0 else g_ref.at[s, pl.ds(cut, depth - cut)]
 
-    g_ref[0] = wout_ref[...]
     ag = Gather(w, mail, view, rsem)
-    ag.start()
+    loads[1].wait()
+    ag.own_x(0)
+    ag.own_y(0)
+    ag.own_y(1)
+    for cp in loads[2:]:
+        cp.wait()
 
     ext_ref[16:, :] = x_ref[...].astype(f32)
     mail.got(tail_ref, tsem.at[0], sib)
@@ -183,10 +198,12 @@
     jj = lax.broadcasted_iota(jnp.int32, (toks, toks), 1)
     low = ii >= jj
     lowf = jnp.where(low, 1.0, 0.0)
-    cum = jnp.dot(lowf, ld_ref[...], precision=highest, preferred_element_type=f32)
-    cum_t = lax.dot_general(
-        ld_ref[...], jnp.where(ii <= jj, 1.0, 0.0), (((0,), (0,)), ((), ())),
+    cum = lax.dot_general(
+        lowf, ld_ref[...], (((1,), (1,)), ((), ())),
         precision=highest, preferred_element_type=f32,
+    )
+    cum_t = jnp.dot(
+        ld_ref[...], jnp.where(ii <= jj, 1.0, 0.0), precision=highest, preferred_element_type=f32
     )
     eh = lax.broadcasted_iota(jnp.int32, (heads, chans), 0) * HEAD
     ec = lax.broadcasted_iota(jnp.int32, (heads, chans), 1)
@@ -263,11 +280,14 @@
     by_rows(join)
     for i, dx in enumerate((1, 3, 2)):
         mail.send(s2_ref.at[w.x], s2_ref.at[w.x], tsem.at[1 + NX - dx], w.tok_dev(dx, 0, 0))
-    for p in range(2, 5):
+    ag.own_x(1)
+    for part in (0, 1):
+        ag.put((0, 0, 0), part, (0, 0, 1), (0, 0, 1))
+    for p in range(2, heads // 2):
         inside(p)
-    ag.y_in()
-    for p in range(5, heads // 2):
-        inside(p)
+    ag.y_in(0)
+    ag.y_in(1)
+    ag.x_in(1)
     for dx in (1, 3, 2):
         mail.got(s2_ref.at[lax.rem(w.x + dx, NX)], tsem.at[1 + dx], w.tok_dev(dx, 0, 0))
     decs = [decay_of(s2_ref[k, DEC, :]) for k in range(NX)]
@@ -286,8 +306,8 @@
 
     by_rows(row_scan)
     mail.send(r_out_ref.at[0], r_in_ref, usem.at[1], w.tok_dev(0, 1, 0))
-    for dx in (1, 3, 2):
-        ag.x_in(dx)
+    ag.x_in(3)
+    ag.x_in(2)
     mail.got(r_in_ref, usem.at[1], w.tok_dev(0, 1, 0))
     lower = w.y > 0
 
@@ -320,33 +340,34 @@
             scan_ref[...], g_ref[slot(dx, dy, dc)], preferred_element_type=f32
         ).astype(bf16)
 
+    rows = hid_ref.shape[0]
+
+    def mine(e):
+        return pl.ds(pl.multiple_of(e * rows, rows), rows)
+
+    def out(dx, dy):
+        chip = (w.tok(dx, dy, 0) // 2) * 2 * width
+        cols = pl.ds(pl.multiple_of(chip, 2 * width), 2 * width)
+        for k in range(1, NE):
+            mail.send(
+                part_ref.at[mine(w.exp(k)), cols], rec_ref.at[k - 1, :, cols], esem.at[k - 1],
+                {"expert": w.exp(k)},
+            )
+
+    def pair(dx, dy):
+        mult(dx, dy, 0)
+        ag.sib_in(dx, dy)
+        mult(dx, dy, 1)
+        out(dx, dy)
+
     for dx in (1, 3, 2):
         ag.x_in_late(dx)
-    mult(0, 0, 0)
-    ag.sib_in(0, 0)
-    mult(0, 0, 1)
-    mult(0, 1, 0)
-    ag.sib_in(0, 1)
-    mult(0, 1, 1)
-    for dx in (1, 3, 2):
-        mult(dx, 0, 0)
-        ag.sib_in(dx, 0)
-        mult(dx, 0, 1)
+    for d in ((0, 0), (0, 1), (1, 0), (3, 0), (2, 0)):
+        pair(*d)
     for dx in (1, 3, 2):
         ag.far_in(dx)
-        mult(dx, 1, 0)
     for dx in (1, 3, 2):
-        ag.sib_in(dx, 1)
-        mult(dx, 1, 1)
-    rows = hid_ref.shape[0]
-
-    def mine(e):
-        return pl.ds(pl.multiple_of(e * rows, rows), rows)
-
-    for k in range(1, NE):
-        mail.send(
-            part_ref.at[mine(w.exp(k))], rec_ref.at[k - 1], esem.at[k - 1], {"expert": w.exp(k)}
-        )
+        pair(dx, 1)
     total = part_ref[mine(w.e), :].astype(f32)
     for k in range(1, NE):
         mail.got(rec_ref.at[k - 1], esem.at[k - 1], {"expert": w.exp(k)})
@@ -362,14 +383,16 @@
     toks, chans = x_in.shape
     model, n_state = gain.shape[1], b_proj.shape[1]
     half = chans // 2
+    small = (x_in, conv_w, b_proj, c_proj, log_decay, d_skip, gain)
     vm = pl.BlockSpec(memory_space=pltpu.VMEM)
     dma = pltpu.SemaphoreType.DMA
     return pl.pallas_call(
         mixer_kernel,
         out_shape=[jax.ShapeDtypeStruct((rows, model), bf16)] * 2,
-        in_specs=[vm] * 8,
+        in_specs=[pl.BlockSpec(memory_space=pl.ANY)] * 8,
         out_specs=[vm] * 2,
         scratch_shapes=[
+            *[pltpu.VMEM(a.shape, a.dtype) for a in small],
             pltpu.VMEM((16, depth, width), bf16),
             pltpu.VMEM((toks, model), bf16),
             pltpu.VMEM((NE - 1, rows, model), bf16),
@@ -386,14 +409,15 @@
             pltpu.VMEM((2, n_state, half), bf16),
             pltpu.VMEM((n_state, half), bf16),
             pltpu.VMEM((toks, chans), bf16),
-            dma((AG_SENDS + NE - 1 + 7,)),
+            dma((AG_SENDS + 8 * (NE - 1) + 7,)),
             dma((16, 2)),
             dma((NE - 1,)),
             dma((1 + NX,)),
             dma((3,)),
+            dma((8,)),
         ],
         compiler_params=pltpu.CompilerParams(
-            collective_id=1, has_side_effects=True, vmem_limit_bytes=40 * 2**20
+            collective_id=1, has_side_effects=True, vmem_limit_bytes=56 * 2**20
         ),
         cost_estimate=pl.CostEstimate(
             flops=2 * toks * depth * model, bytes_accessed=20 * 2**20, transcendentals=0
@@ -405,7 +429,7 @@
 def expert_kernel(
     nrm_ref, rt_ref, hid_ref, wr_ref, we_ref, out_ref,
     wv_ref, n_ref, r_ref, g_ref, a_ref, o_ref, sib_ref, yp_ref, yq_ref, xp_ref, xq_ref,
-    con_ref, rec_ref,
+    con_ref, rec_ref, own_ref,
     lsem, ssem, nsem, tsem, gsem, bsem, psem, qsem, fsem, esem,
 ):
     w = Where()
@@ -419,6 +443,9 @@
     loads = [pltpu.make_async_copy(we_ref.at[0, i], wv_ref.at[i], lsem.at[i]) for i in range(3)]
     for cp in loads:
         cp.start()
+    lane = lax.broadcasted_iota(jnp.int32, (rows, 128), 1)
+    ids = rt_ref[...].astype(f32)
+    own_ref[...] = jnp.where(lane == 0, ids[:, 0:1], ids[:, 1:2]).astype(bf16)
     greet(w)
 
     def of(e):
@@ -426,14 +453,16 @@
 
     me = of(w.e)
     for k in range(1, NE):
-        mail.send(rt_ref, r_ref.at[me], tsem.at[k - 1], {"expert": w.exp(k)})
-        mail.send(nrm_ref, n_ref.at[me], nsem.at[k - 1], {"expert": w.exp(k)})
+        mail.send(own_ref, r_ref.at[me], tsem.at[k - 1], {"expert": w.exp(k)})
+    for i, cols in enumerate((P, Q)):
+        for k in range(1, NE):
+            mail.send(
+                nrm_ref.at[:, cols], n_ref.at[me, cols], nsem.at[i, k - 1], {"expert": w.exp(k)}
+            )
     n_ref[me, :] = nrm_ref[...]
-    r_ref[me, :] = rt_ref[...]
+    r_ref[me, :] = own_ref[...]
     for k in range(1, NE):
-        frm = of(w.exp(NE - k))
-        mail.got(r_ref.at[frm], tsem.at[k - 1], {"expert": w.exp(k)})
-        mail.got(n_ref.at[frm], nsem.at[k - 1], {"expert": w.exp(k)})
+        mail.got(r_ref.at[of(w.exp(NE - k))], tsem.at[k - 1], {"expert": w.exp(k)})
 
     ii = lax.broadcasted_iota(jnp.int32, (toks, toks), 0)
     jj = lax.broadcasted_iota(jnp.int32, (toks, toks), 1)
@@ -447,17 +476,20 @@
     want = lax.broadcasted_iota(jnp.int32, (cap, toks), 0).astype(f32)
     sel_f = jnp.where(want == rank, 1.0, 0.0) * hit_row
     sel = sel_f.astype(bf16)
-    for b in range(4):
-        cols = pl.ds(b * (model // 4), model // 4)
-        g_ref[0, :, cols] = jnp.dot(sel, n_ref[:, cols], preferred_element_type=f32).astype(bf16)
 
     def view(s, part):
         return g_ref.at[s, :, Q if part else P]
 
     ag = Gather(w, mail, view, gsem)
-    ag.start()
-
-    logits = jnp.dot(n_ref[...], wr_ref[...], preferred_element_type=f32)
+    for i, cols in enumerate((P, Q)):
+        for k in range(1, NE):
+            mail.got(n_ref.at[of(w.exp(NE - k)), cols], nsem.at[i, k - 1], {"expert": w.exp(k)})
+        g_ref[0, :, cols] = jnp.dot(sel, n_ref[:, cols], preferred_element_type=f32).astype(bf16)
+        ag.start(i)
+
+    logits = lax.dot_general(
+        n_ref[...], wr_ref[...], (((1,), (1,)), ((), ())), preferred_element_type=f32
+    )
     lane = lax.broadcasted_iota(jnp.int32, logits.shape, 1).astype(f32)
     s1 = jax.nn.sigmoid(jnp.sum(jnp.where(lane == r1, logits, 0.0), axis=1, keepdims=True))
     s2 = jax.nn.sigmoid(jnp.sum(jnp.where(lane == r2, logits, 0.0), axis=1, keepdims=True))
@@ -467,16 +499,11 @@
 
     def compute(group):
         xs = pl.ds(group * 4, 4)
-        tile = 256
-
-        @pl.loop(0, hidden // tile)
-        def _(i):
-            cols = pl.ds(pl.multiple_of(i * tile, tile), tile)
-            xg = g_ref[xs].reshape(4 * cap, model)
-            gv = jnp.dot(xg, wv_ref[0, :, cols], preferred_element_type=f32)
-            uv = jnp.dot(xg, wv_ref[1, :, cols], preferred_element_type=f32)
-            a_ref[:, cols] = (gv / (1.0 + jnp.exp(-gv)) * uv).astype(bf16)
-
+        tile = 1024
+        xg = g_ref[xs].reshape(4 * cap, model)
+        gv = jnp.dot(xg, wv_ref[0], preferred_element_type=f32)
+        uv = jnp.dot(xg, wv_ref[1], preferred_element_type=f32)
+        a_ref[...] = (gv / (1.0 + jnp.exp(-gv)) * uv).astype(bf16)
         if group == 0:
             loads[2].wait()
 
@@ -528,7 +555,11 @@
         if dy == 1:
             mail.send(o_ref.at[slot(0, 1, 0), :, Q], yq_ref, fsem.at[3], w.tok_dev(0, 1, 0))
 
-    ag.y_in()
+    ag.y_in(0)
+    ag.x_in(1)
+    ag.x_in(3)
+    ag.y_in(1)
+    ag.x_in(2)
     ag.sib_in(0, 0)
     ag.sib_in(0, 1)
     loads[0].wait()
@@ -536,56 +567,60 @@
     compute(0)
     pair_out(0)
     for dx in (1, 3, 2):
-        ag.x_in(dx)
-    for dx in (1, 3):
         ag.x_in_late(dx)
-    ag.x_in_late(2)
     ag.sib_in(1, 0)
     ag.sib_in(3, 0)
     compute(1)
     pair_out(1)
-    for dx in (2, 1, 3):
-        ag.far_in(dx)
     pair_in(0)
+    ag.far_in(1)
     ag.sib_in(2, 0)
-    ag.sib_in(2, 1)
+    ag.sib_in(1, 1)
     compute(2)
     pair_out(2)
+    ag.far_in(3)
+    ag.far_in(2)
     pair_in(1)
-    ag.sib_in(1, 1)
     ag.sib_in(3, 1)
+    ag.sib_in(2, 1)
     compute(3)
     pair_out(3)
     pair_in(2)
+    y_sum(1)
+    pair_in(3)
+    x_sum(1)
+    y_sum(3)
     y_sum(2)
-    pair_in(3)
-    y_sum(1)
-    y_sum(3)
-    x_sum(1)
     y_sum(0)
     x_sum(0)
 
-    for b in range(3):
-        mail.got(xp_ref.at[b], fsem.at[b], w.tok_dev(1, 0, 0))
-    mail.got(yq_ref, fsem.at[3], w.tok_dev(0, 1, 0))
-
-    def final(cols, srcs):
+    def final(i, cols, srcs):
         v = o_ref[0, :, cols].astype(f32)
         for src in srcs:
             v = v + src.astype(f32)
-        return lax.dot_general(
+        con_ref[:, cols] = lax.dot_general(
             sel, (v * gate_col).astype(bf16), (((0,), (0,)), ((), ())), preferred_element_type=f32
         ).astype(bf16)
-
-    con_ref[:, P] = final(P, [xp_ref[b] for b in range(3)])
-    con_ref[:, Q] = final(Q, [yq_ref[...]])
-    for k in range(1, NE):
-        mail.send(con_ref.at[of(w.exp(k))], rec_ref.at[k - 1], esem.at[k - 1], {"expert": w.exp(k)})
-    total = hid_ref[...].astype(f32) + con_ref[me, :].astype(f32)
-    for k in range(1, NE):
-        mail.got(rec_ref.at[k - 1], esem.at[k - 1], {"expert": w.exp(k)})
-        total = total + rec_ref[k - 1].astype(f32)
-    out_ref[...] = total.astype(bf16)
+        for k in range(1, NE):
+            mail.send(
+                con_ref.at[of(w.exp(k)), cols], rec_ref.at[k - 1, :, cols], esem.at[i, k - 1],
+                {"expert": w.exp(k)},
+            )
+
+    def finish(i, cols):
+        total = hid_ref[:, cols].astype(f32) + con_ref[me, cols].astype(f32)
+        for k in range(1, NE):
+            mail.got(rec_ref.at[k - 1, :, cols], esem.at[i, k - 1], {"expert": w.exp(k)})
+            total = total + rec_ref[k - 1, :, cols].astype(f32)
+        out_ref[:, cols] = total.astype(bf16)
+
+    mail.got(yq_ref, fsem.at[3], w.tok_dev(0, 1, 0))
+    final(1, Q, [yq_ref[...]])
+    for b in range(3):
+        mail.got(xp_ref.at[b], fsem.at[b], w.tok_dev(1, 0, 0))
+    final(0, P, [xp_ref[b] for b in range(3)])
+    finish(1, Q)
+    finish(0, P)
     mail.drain()
 
 
@@ -595,7 +630,7 @@
     toks, cap = rows * NE, 80
     cut = model * 5 // 8
     vm = pl.BlockSpec(memory_space=pltpu.VMEM)
-    sends = 2 * (NE - 1) + AG_SENDS + 8 + 4 + 6 + 3 + 1 + NE - 1
+    sends = 5 * (NE - 1) + AG_SENDS + 8 + 4 + 6 + 3 + 1
     dma = pltpu.SemaphoreType.DMA
     return pl.pallas_call(
         expert_kernel,
@@ -616,8 +651,9 @@
             pltpu.VMEM((6, cap, model - cut), bf16),
             pltpu.VMEM((toks, model), bf16),
             pltpu.VMEM((NE - 1, rows, model), bf16),
-            dma((3,)), dma((sends,)), dma((NE - 1,)), dma((NE - 1,)), dma((16, 2)), dma((8,)),
-            dma((4,)), dma((6,)), dma((4,)), dma((NE - 1,)),
+            pltpu.VMEM((rows, 128), bf16),
+            dma((3,)), dma((sends,)), dma((2, NE - 1)), dma((NE - 1,)), dma((16, 2)), dma((8,)),
+            dma((4,)), dma((6,)), dma((4,)), dma((2, NE - 1)),
         ],
         compiler_params=pltpu.CompilerParams(
             collective_id=2, has_side_effects=True, vmem_limit_bytes=60 * 2**20
@@ -633,11 +669,10 @@
     x_in, conv_w, b_proj, c_proj, log_decay, d_skip, w_out, norm_gain, w_router, w_expert, route_ids
 ):
     rows, model = route_ids.shape[1], norm_gain.shape[0]
-    route = jnp.pad(route_ids[0].astype(bf16), ((0, 0), (0, 126)))
     hidden, normed = mixer(
-        x_in, conv_w, b_proj, c_proj, log_decay, d_skip[None], w_out, norm_gain[None], rows
-    )
-    layer_out = expert_layer(normed, route, hidden, w_router, w_expert)
+        x_in, conv_w, b_proj, c_proj, log_decay.T, d_skip[None], w_out, norm_gain[None], rows
+    )
+    layer_out = expert_layer(normed, route_ids[0], hidden, w_router.T, w_expert)
     return layer_out.reshape(1, rows, model)
 
 

time: 246 us -> 202 us (0.82)
  Pallas kernels: 232 us -> 199 us
  local copies, waits for them, and re-layouts: 12.1 us -> 2.92 us
    pallas_call x1, Pallas kernels: 78.8 us -> 61.2 us  [mixer(): pl.pallas_call(mixer_kernel, out_shape=[jax.ShapeDtypeStruct((rows, model...]
    pallas_call x1, Pallas kernels: 153 us -> 138 us  [expert_layer(): pl.pallas_call(expert_kernel, out_shape=jax.ShapeDtypeStruct((rows, model...]
    unnamed x21 -> x1, local copies, waits for them, and re-layouts: 11.4 us -> 1.57 us
where the time goes in v3:
time: 202 us
  Pallas kernels  199 us (99%)
  local copies, waits for them, and re-layouts  2.92 us (1%)
    pallas_call x1, Pallas kernels, expert_layer(): pl.pallas_call(expert_kernel, out_shape=jax.ShapeDtypeStruct((rows, model...  138 us
    pallas_call x1, Pallas kernels, mixer(): pl.pallas_call(mixer_kernel, out_shape=[jax.ShapeDtypeStruct((rows, model...  61.2 us

profile of v3, /device:TPU:6, one launch (start us, length us, event | category | flops | bytes accessed | tf_op | source)
XLA Modules:
  0.0 202.1 jit_solution(15735169218188053010)
XLA Ops:
  0.0 1.4 copy.12.rt_ref
  1.4 61.2 %mixer.1 = (bf16[16,4096]{1,0:T(8,128)(2,1)}, bf16[16,4096]{1,0:T(8,128)(2,1)}) custom-call(bf16[128,1024]{1,0:T(8,128)(2,1)} %x_hbm.1, f32[4,1024]{1,0:T(4,128)} %cw_hbm.1, bf16[128,128]{1,0:T(8,128)(2,1)} %b_hbm.1, bf16[128,128]{1,0:T(8,128)(2,1)} %c_hbm.1, f32[16,128]{1,0:T(8,128)} %bitcast.10, f32[1,16]{1,0:T(1,128)} %bitcast.11, ...), custom_call_target="tpu_custom_call" | custom-call | flops 1073741824 | bytes 20971520 | tf_op jit(solution)/shard_map/mixer/pallas_call | solution.py:389
  62.6 137.9 %expert_layer.1 = bf16[16,4096]{1,0:T(8,128)(2,1)} custom-call(bf16[16,4096]{1,0:T(8,128)(2,1)} %get-tuple-element.7.nrm_ref, s32[16,2]{1,0:T(8,128)} %copy.12.rt_ref, bf16[16,4096]{1,0:T(8,128)(2,1)} %get-tuple-element.8.hid_ref, bf16[8,4096]{1,0:T(8,128)(2,1)} %bitcast.8, bf16[1,3,4096,768]{3,2,1,0:T(8,128)(2,1)} %we_ref.1), custom_call_target="tpu_custom_call" | custom-call | flops 24159191040 | bytes 20971520 | tf_op jit(solution)/shard_map/expert_layer/pallas_call | solution.py:635
  200.5 1.6 copy.14

commit v4 on v3

--- a/solution.py
+++ b/solution.py
@@ -92,48 +92,38 @@
         s = slot(dx, dy, dc)
         self.mail.got(self.view(s, part), self.rsems.at[s, part], self.w.tok_dev(0, 0, 1))
 
-    def start(self, part):
-        self.own_y(part)
-        self.own_x(part)
-        self.put((0, 0, 0), part, (0, 0, 1), (0, 0, 1))
-
     def own_y(self, part):
         self.put((0, 0, 0), part, (0, 1, 0), (0, 1, 0))
 
-    def own_x(self, part):
-        for dx in (1, 3, 2):
-            self.put((0, 0, 0), part, (dx, 0, 0), (-dx, 0, 0))
-
-    def sib(self, dx, dy, part):
+    def own_sib(self, part):
+        self.put((0, 0, 0), part, (0, 0, 1), (0, 0, 1))
+
+    def along_x(self, dy, part):
+        for dx in (1, 3):
+            self.put((0, dy, 0), part, (dx, 0, 0), (-dx, dy, 0))
+
+    def own(self, part):
+        self.own_y(part)
+        self.along_x(0, part)
+        self.own_sib(part)
+
+    def arrive(self, dx, dy, part):
+        self.got(dx, dy, 0, part)
+        on = (3, 1, 3, 1)[part]
+        if dx == (NX - on) and (part > 1 or dy == 0):
+            self.put((dx, dy, 0), part, (on, 0, 0), (2, dy, 0))
+        if part < 2 and dx != 0 and dy == 0:
+            self.put((dx, 0, 0), part, (0, 1, 0), (dx, 1, 0))
+        if part > 1 and dx == 0:
+            self.along_x(1, part)
         self.put((dx, dy, 0), part, (0, 0, 1), (dx, dy, 1))
 
-    def y_in(self, part):
-        self.got(0, 1, 0, part)
-        if part == 1:
-            for dx in (1, 3, 2):
-                self.put((0, 1, 0), 1, (dx, 0, 0), (-dx, 1, 0))
-        self.sib(0, 1, part)
-
-    def x_in(self, dx):
-        self.got(dx, 0, 0, 0)
-        self.put((dx, 0, 0), 0, (0, 1, 0), (dx, 1, 0))
-        self.sib(dx, 0, 0)
-
-    def x_in_late(self, dx):
-        self.got(dx, 0, 0, 1)
-        self.sib(dx, 0, 1)
-
-    def far_in(self, dx):
-        for part in (0, 1):
-            self.got(dx, 1, 0, part)
-            self.sib(dx, 1, part)
-
     def sib_in(self, dx, dy):
-        for part in (0, 1):
+        for part in range(4):
             self.got(dx, dy, 1, part)
 
 
-AG_SENDS = 2 + 3 + 3 + 2 + (3 + 2) + 3 * 2 + 3 + 3 * 2
+AG_SENDS = 60
 
 
 def rms(hid, gain):
@@ -165,7 +155,7 @@
     half = chans // 2
     n_state = b_ref.shape[1]
     depth, width = wout_ref.shape
-    cut = depth * 5 // 8
+    cut = depth // 4
     sib = w.tok_dev(0, 0, 1)
     greet(w, behind=True)
     loads[0].wait()
@@ -174,13 +164,14 @@
     )
 
     def view(s, part):
-        return g_ref.at[s, pl.ds(0, cut)] if part == 0 else g_ref.at[s, pl.ds(cut, depth - cut)]
+        return g_ref.at[s, pl.ds(part * cut, cut)]
 
     ag = Gather(w, mail, view, rsem)
     loads[1].wait()
-    ag.own_x(0)
-    ag.own_y(0)
-    ag.own_y(1)
+    for part in (0, 1):
+        ag.along_x(0, part)
+    for part in (2, 0, 3, 1):
+        ag.own_y(part)
     for cp in loads[2:]:
         cp.wait()
 
@@ -280,14 +271,14 @@
     by_rows(join)
     for i, dx in enumerate((1, 3, 2)):
         mail.send(s2_ref.at[w.x], s2_ref.at[w.x], tsem.at[1 + NX - dx], w.tok_dev(dx, 0, 0))
-    ag.own_x(1)
-    for part in (0, 1):
-        ag.put((0, 0, 0), part, (0, 0, 1), (0, 0, 1))
+    for part in (2, 3):
+        ag.along_x(0, part)
+    for part in range(4):
+        ag.own_sib(part)
     for p in range(2, heads // 2):
         inside(p)
-    ag.y_in(0)
-    ag.y_in(1)
-    ag.x_in(1)
+    for d in ((1, 0, 0), (3, 0, 0), (0, 1, 2)):
+        ag.arrive(*d)
     for dx in (1, 3, 2):
         mail.got(s2_ref.at[lax.rem(w.x + dx, NX)], tsem.at[1 + dx], w.tok_dev(dx, 0, 0))
     decs = [decay_of(s2_ref[k, DEC, :]) for k in range(NX)]
@@ -306,8 +297,8 @@
 
     by_rows(row_scan)
     mail.send(r_out_ref.at[0], r_in_ref, usem.at[1], w.tok_dev(0, 1, 0))
-    ag.x_in(3)
-    ag.x_in(2)
+    for d in ((1, 0, 1), (3, 0, 1), (0, 1, 3), (0, 1, 0), (0, 1, 1), (2, 0, 0), (2, 0, 1)):
+        ag.arrive(*d)
     mail.got(r_in_ref, usem.at[1], w.tok_dev(0, 1, 0))
     lower = w.y > 0
 
@@ -323,6 +314,10 @@
     by_rows(enter)
     mail.send(hand_ref, sin_ref.at[w.c], usem.at[2], sib)
 
+    for part in (2, 3):
+        for d in ((1, 0, part), (3, 0, part)):
+            ag.arrive(*d)
+
     def close(h):
         for b in range(2):
             cols = pl.ds(pl.multiple_of(h * half + b * (half // 2), half // 2), half // 2)
@@ -360,14 +355,18 @@
         mult(dx, dy, 1)
         out(dx, dy)
 
-    for dx in (1, 3, 2):
-        ag.x_in_late(dx)
+    for part in (2, 3):
+        for d in ((1, 1, part), (3, 1, part), (2, 0, part)):
+            ag.arrive(*d)
     for d in ((0, 0), (0, 1), (1, 0), (3, 0), (2, 0)):
         pair(*d)
-    for dx in (1, 3, 2):
-        ag.far_in(dx)
-    for dx in (1, 3, 2):
+    for dx in (1, 3):
+        for part in (0, 1):
+            ag.arrive(dx, 1, part)
         pair(dx, 1)
+    for part in (2, 3, 0, 1):
+        ag.arrive(2, 1, part)
+    pair(2, 1)
     total = part_ref[mine(w.e), :].astype(f32)
     for k in range(1, NE):
         mail.got(rec_ref.at[k - 1], esem.at[k - 1], {"expert": w.exp(k)})
@@ -410,7 +409,7 @@
             pltpu.VMEM((n_state, half), bf16),
             pltpu.VMEM((toks, chans), bf16),
             dma((AG_SENDS + 8 * (NE - 1) + 7,)),
-            dma((16, 2)),
+            dma((16, 4)),
             dma((NE - 1,)),
             dma((1 + NX,)),
             dma((3,)),
@@ -438,7 +437,7 @@
     cap = g_ref.shape[1]
     hidden = wv_ref.shape[2]
     toks = n_ref.shape[0]
-    cut = model * 5 // 8
+    cut = model // 2
     P, Q = pl.ds(0, cut), pl.ds(cut, model - cut)
     loads = [pltpu.make_async_copy(we_ref.at[0, i], wv_ref.at[i], lsem.at[i]) for i in range(3)]
     for cp in loads:
@@ -454,10 +453,12 @@
     me = of(w.e)
     for k in range(1, NE):
         mail.send(own_ref, r_ref.at[me], tsem.at[k - 1], {"expert": w.exp(k)})
-    for i, cols in enumerate((P, Q)):
+    quarter = [pl.ds(i * (model // 4), model // 4) for i in range(4)]
+    for i in (0, 2, 1, 3):
         for k in range(1, NE):
             mail.send(
-                nrm_ref.at[:, cols], n_ref.at[me, cols], nsem.at[i, k - 1], {"expert": w.exp(k)}
+                nrm_ref.at[:, quarter[i]], n_ref.at[me, quarter[i]], nsem.at[i, k - 1],
+                {"expert": w.exp(k)},
             )
     n_ref[me, :] = nrm_ref[...]
     r_ref[me, :] = own_ref[...]
@@ -478,14 +479,24 @@
     sel = sel_f.astype(bf16)
 
     def view(s, part):
-        return g_ref.at[s, :, Q if part else P]
+        return g_ref.at[s, :, quarter[part]]
 
     ag = Gather(w, mail, view, gsem)
-    for i, cols in enumerate((P, Q)):
+
+    def feed(i):
+        cols = quarter[i]
         for k in range(1, NE):
             mail.got(n_ref.at[of(w.exp(NE - k)), cols], nsem.at[i, k - 1], {"expert": w.exp(k)})
         g_ref[0, :, cols] = jnp.dot(sel, n_ref[:, cols], preferred_element_type=f32).astype(bf16)
-        ag.start(i)
+        ag.own(i)
+
+    feed(0)
+    feed(2)
+    ag.arrive(1, 0, 0)
+    ag.arrive(3, 0, 0)
+    feed(1)
+    ag.arrive(0, 1, 2)
+    feed(3)
 
     logits = lax.dot_general(
         n_ref[...], wr_ref[...], (((1,), (1,)), ((), ())), preferred_element_type=f32
@@ -497,15 +508,14 @@
     gate_row = jnp.sum(gate * eye, axis=0, keepdims=True)
     gate_col = jnp.sum(sel_f * gate_row, axis=1, keepdims=True)
 
-    def compute(group):
-        xs = pl.ds(group * 4, 4)
-        tile = 1024
-        xg = g_ref[xs].reshape(4 * cap, model)
+    def gate_up(group):
+        xg = g_ref[pl.ds(group * 4, 4)].reshape(4 * cap, model)
         gv = jnp.dot(xg, wv_ref[0], preferred_element_type=f32)
         uv = jnp.dot(xg, wv_ref[1], preferred_element_type=f32)
         a_ref[...] = (gv / (1.0 + jnp.exp(-gv)) * uv).astype(bf16)
-        if group == 0:
-            loads[2].wait()
+
+    def down(group):
+        tile = 1024
 
         @pl.loop(0, model // tile)
         def _(i):
@@ -513,7 +523,7 @@
             o = lax.dot_general(
                 a_ref[...], wv_ref[2, cols, :], (((1,), (1,)), ((), ())), preferred_element_type=f32
             )
-            o_ref[xs, :, cols] = o.astype(bf16).reshape(4, cap, tile)
+            o_ref[pl.ds(group * 4, 4), :, cols] = o.astype(bf16).reshape(4, cap, tile)
 
     def add(dst, cols, *srcs):
         @pl.loop(0, cap // 16)
@@ -555,37 +565,47 @@
         if dy == 1:
             mail.send(o_ref.at[slot(0, 1, 0), :, Q], yq_ref, fsem.at[3], w.tok_dev(0, 1, 0))
 
-    ag.y_in(0)
-    ag.x_in(1)
-    ag.x_in(3)
-    ag.y_in(1)
-    ag.x_in(2)
+    for d in ((1, 0, 1), (3, 0, 1), (2, 0, 0), (0, 1, 3), (0, 1, 0), (0, 1, 1), (2, 0, 1)):
+        ag.arrive(*d)
     ag.sib_in(0, 0)
     ag.sib_in(0, 1)
     loads[0].wait()
     loads[1].wait()
-    compute(0)
+    gate_up(0)
+    for part in (2, 3):
+        ag.arrive(1, 0, part)
+        ag.arrive(3, 0, part)
+    loads[2].wait()
+    down(0)
     pair_out(0)
-    for dx in (1, 3, 2):
-        ag.x_in_late(dx)
     ag.sib_in(1, 0)
     ag.sib_in(3, 0)
-    compute(1)
+    gate_up(1)
+    for part in (2, 3):
+        ag.arrive(1, 1, part)
+        ag.arrive(3, 1, part)
+        ag.arrive(2, 0, part)
+    pair_in(0)
+    down(1)
     pair_out(1)
-    pair_in(0)
-    ag.far_in(1)
+    for part in (0, 1):
+        ag.arrive(1, 1, part)
     ag.sib_in(2, 0)
     ag.sib_in(1, 1)
-    compute(2)
+    gate_up(2)
+    pair_in(1)
+    for part in (0, 1):
+        ag.arrive(3, 1, part)
+    for part in (2, 3, 0, 1):
+        ag.arrive(2, 1, part)
+    down(2)
     pair_out(2)
-    ag.far_in(3)
-    ag.far_in(2)
-    pair_in(1)
     ag.sib_in(3, 1)
     ag.sib_in(2, 1)
-    compute(3)
+    gate_up(3)
+    pair_in(2)
+    down(3)
     pair_out(3)
-    pair_in(2)
     y_sum(1)
     pair_in(3)
     x_sum(1)
@@ -628,9 +648,9 @@
     rows, model = normed.shape
     units = w_expert.shape[3]
     toks, cap = rows * NE, 80
-    cut = model * 5 // 8
+    cut = model // 2
     vm = pl.BlockSpec(memory_space=pltpu.VMEM)
-    sends = 5 * (NE - 1) + AG_SENDS + 8 + 4 + 6 + 3 + 1
+    sends = 7 * (NE - 1) + AG_SENDS + 8 + 4 + 6 + 3 + 1
     dma = pltpu.SemaphoreType.DMA
     return pl.pallas_call(
         expert_kernel,
@@ -652,7 +672,7 @@
             pltpu.VMEM((toks, model), bf16),
             pltpu.VMEM((NE - 1, rows, model), bf16),
             pltpu.VMEM((rows, 128), bf16),
-            dma((3,)), dma((sends,)), dma((2, NE - 1)), dma((NE - 1,)), dma((16, 2)), dma((8,)),
+            dma((3,)), dma((sends,)), dma((4, NE - 1)), dma((NE - 1,)), dma((16, 4)), dma((8,)),
             dma((4,)), dma((6,)), dma((4,)), dma((2, NE - 1)),
         ],
         compiler_params=pltpu.CompilerParams(

time: 202 us -> 188 us (0.931)
  Pallas kernels: 199 us -> 185 us
    pallas_call x1, Pallas kernels: 138 us -> 128 us  [expert_layer(): pl.pallas_call(expert_kernel, out_shape=jax.ShapeDtypeStruct((rows, model...]
    pallas_call x1, Pallas kernels: 61.2 us -> 56.9 us  [mixer(): pl.pallas_call(mixer_kernel, out_shape=[jax.ShapeDtypeStruct((rows, model...]
where the time goes in v4:
time: 188 us
  Pallas kernels  185 us (98%)
  local copies, waits for them, and re-layouts  2.92 us (2%)
    pallas_call x1, Pallas kernels, expert_layer(): pl.pallas_call(expert_kernel, out_shape=jax.ShapeDtypeStruct((rows, model...  128 us
    pallas_call x1, Pallas kernels, mixer(): pl.pallas_call(mixer_kernel, out_shape=[jax.ShapeDtypeStruct((rows, model...  56.9 us

profile of v4, /device:TPU:6, one launch (start us, length us, event | category | flops | bytes accessed | tf_op | source)
XLA Modules:
  0.0 187.8 jit_solution(10005200408992954057)
XLA Ops:
  0.0 1.4 copy.12.rt_ref
  1.4 56.9 %mixer.1 = (bf16[16,4096]{1,0:T(8,128)(2,1)}, bf16[16,4096]{1,0:T(8,128)(2,1)}) custom-call(bf16[128,1024]{1,0:T(8,128)(2,1)} %x_hbm.1, f32[4,1024]{1,0:T(4,128)} %cw_hbm.1, bf16[128,128]{1,0:T(8,128)(2,1)} %b_hbm.1, bf16[128,128]{1,0:T(8,128)(2,1)} %c_hbm.1, f32[16,128]{1,0:T(8,128)} %bitcast.10, f32[1,16]{1,0:T(1,128)} %bitcast.11, ...), custom_call_target="tpu_custom_call" | custom-call | flops 1073741824 | bytes 20971520 | tf_op jit(solution)/shard_map/mixer/pallas_call | solution.py:388
  58.3 127.9 %expert_layer.1 = bf16[16,4096]{1,0:T(8,128)(2,1)} custom-call(bf16[16,4096]{1,0:T(8,128)(2,1)} %get-tuple-element.7.nrm_ref, s32[16,2]{1,0:T(8,128)} %copy.12.rt_ref, bf16[16,4096]{1,0:T(8,128)(2,1)} %get-tuple-element.8.hid_ref, bf16[8,4096]{1,0:T(8,128)(2,1)} %bitcast.8, bf16[1,3,4096,768]{3,2,1,0:T(8,128)(2,1)} %we_ref.1), custom_call_target="tpu_custom_call" | custom-call | flops 24159191040 | bytes 20971520 | tf_op jit(solution)/shard_map/expert_layer/pallas_call | solution.py:655
  186.2 1.6 copy.14

commit v5 on v4

--- a/solution.py
+++ b/solution.py
@@ -11,7 +11,7 @@
 MESH = pl.DeviceIdType.MESH
 bf16, f32 = jnp.bfloat16, jnp.float32
 NX, NE = 4, 8
-ORDER = [(0, 0), (0, 1), (1, 0), (3, 0), (2, 0), (1, 1), (3, 1), (2, 1)]
+ORDER = [(0, 0), (0, 1), (1, 0), (3, 0), (2, 0), (2, 1), (1, 1), (3, 1)]
 PLACE = {d: i for i, d in enumerate(ORDER)}
 
 
@@ -427,9 +427,9 @@
 
 def expert_kernel(
     nrm_ref, rt_ref, hid_ref, wr_ref, we_ref, out_ref,
-    wv_ref, n_ref, r_ref, g_ref, a_ref, o_ref, sib_ref, yp_ref, yq_ref, xp_ref, xq_ref,
+    wv_ref, n_ref, r_ref, g_ref, a_ref, o_ref, sib_ref, yp_ref, yq_ref, xf_ref, xr_ref, sum_ref,
     con_ref, rec_ref, own_ref,
-    lsem, ssem, nsem, tsem, gsem, bsem, psem, qsem, fsem, esem,
+    lsem, ssem, nsem, tsem, gsem, bsem, psem, qsem, rsem, fsem, esem,
 ):
     w = Where()
     mail = Mail(ssem)
@@ -444,7 +444,13 @@
         cp.start()
     lane = lax.broadcasted_iota(jnp.int32, (rows, 128), 1)
     ids = rt_ref[...].astype(f32)
-    own_ref[...] = jnp.where(lane == 0, ids[:, 0:1], ids[:, 1:2]).astype(bf16)
+    same = lax.broadcasted_iota(jnp.int32, (rows, rows), 0) == lax.broadcasted_iota(
+        jnp.int32, (rows, rows), 1
+    )
+    cols = [
+        jnp.sum(jnp.where(same, ids[k : k + 1, :], 0.0), axis=1, keepdims=True) for k in (0, 1)
+    ]
+    own_ref[...] = jnp.where(lane == 0, cols[0], cols[1]).astype(bf16)
     greet(w)
 
     def of(e):
@@ -525,14 +531,17 @@
             )
             o_ref[pl.ds(group * 4, 4), :, cols] = o.astype(bf16).reshape(4, cap, tile)
 
-    def add(dst, cols, *srcs):
+    def add(dst, cols, *srcs, out=None):
         @pl.loop(0, cap // 16)
         def _(i):
             r = pl.ds(pl.multiple_of(i * 16, 16), 16)
             v = o_ref[dst, r, cols].astype(f32)
             for src in srcs:
                 v = v + src(r).astype(f32)
-            o_ref[dst, r, cols] = v.astype(bf16)
+            if out is None:
+                o_ref[dst, r, cols] = v.astype(bf16)
+            else:
+                out[r, :] = v
 
     def pair_out(group):
         for p in (0, 1):
@@ -547,23 +556,57 @@
             add(i * 2, slice(None), lambda r, i=i: sib_ref[i, r, :])
             if dy == 1:
                 mail.send(o_ref.at[i * 2, :, P], yp_ref.at[dx], psem.at[dx], w.tok_dev(0, 1, 0))
-            if dx != 0:
-                b = (NX - dx - 1) * 2 + dy
-                mail.send(o_ref.at[i * 2, :, Q], xq_ref.at[b], qsem.at[b], w.tok_dev(dx, 0, 0))
+            spread(dx, dy, 2)
+
+    def lot(dy, part):
+        return (dy if part > 1 else 2) * 2 + part % 2
+
+    def pass_on(dx, dy, part, to, relayed=False):
+        i = lot(dy, part)
+        if relayed:
+            dst, sem = xr_ref.at[i], rsem.at[i]
+        else:
+            side = 0 if to == 1 else 1
+            dst, sem = xf_ref.at[i * 2 + side], qsem.at[i * 2 + side]
+        mail.send(o_ref.at[slot(dx, dy, 0), :, quarter[part]], dst, sem, w.tok_dev(to, 0, 0))
+
+    def spread(dx, dy, part):
+        if dx == 2:
+            pass_on(2, dy, part, 1, True)
+            pass_on(2, dy, part + 1, 3, True)
+        if dx == 1:
+            pass_on(1, dy, part + 1, 1)
+        if dx == 3:
+            pass_on(3, dy, part, 3)
+
+    def relay(dy, part):
+        for p, to in ((part, 1), (part + 1, 3)):
+            i = lot(dy, p)
+            mail.got(xr_ref.at[i], rsem.at[i], w.tok_dev(1, 0, 0))
+            add(slot(to, dy, 0), quarter[p], lambda r, i=i: xr_ref[i, r, :])
+            pass_on(to, dy, p, to)
+
+    def x_in(dy, part):
+        for p in (part, part + 1):
+            for side in (0, 1):
+                i = lot(dy, p) * 2 + side
+                mail.got(xf_ref.at[i], qsem.at[i], w.tok_dev(1, 0, 0))
 
     def y_sum(dx):
         mail.got(yp_ref.at[dx], psem.at[dx], w.tok_dev(0, 1, 0))
         add(slot(dx, 0, 0), P, lambda r: yp_ref[dx, r, :])
-        if dx != 0:
-            b = NX - dx - 1
-            mail.send(o_ref.at[slot(dx, 0, 0), :, P], xp_ref.at[b], fsem.at[b], w.tok_dev(dx, 0, 0))
+        spread(dx, 0, 0)
 
     def x_sum(dy):
-        for b in range(3):
-            mail.got(xq_ref.at[b * 2 + dy], qsem.at[b * 2 + dy], w.tok_dev(1, 0, 0))
-        add(slot(0, dy, 0), Q, *[lambda r, b=b: xq_ref[b * 2 + dy, r, :] for b in range(3)])
+        x_in(dy, 2)
+        for p in (2, 3):
+            i = lot(dy, p) * 2
+            add(
+                slot(0, dy, 0), quarter[p],
+                lambda r, i=i: xf_ref[i, r, :], lambda r, i=i: xf_ref[i + 1, r, :],
+            )
         if dy == 1:
-            mail.send(o_ref.at[slot(0, 1, 0), :, Q], yq_ref, fsem.at[3], w.tok_dev(0, 1, 0))
+            mail.send(o_ref.at[slot(0, 1, 0), :, Q], yq_ref, fsem.at[0], w.tok_dev(0, 1, 0))
 
     for d in ((1, 0, 1), (3, 0, 1), (2, 0, 0), (0, 1, 3), (0, 1, 0), (0, 1, 1), (2, 0, 1)):
         ag.arrive(*d)
@@ -590,34 +633,39 @@
     pair_out(1)
     for part in (0, 1):
         ag.arrive(1, 1, part)
-    ag.sib_in(2, 0)
-    ag.sib_in(1, 1)
-    gate_up(2)
-    pair_in(1)
-    for part in (0, 1):
         ag.arrive(3, 1, part)
     for part in (2, 3, 0, 1):
         ag.arrive(2, 1, part)
+    ag.sib_in(2, 0)
+    ag.sib_in(2, 1)
+    gate_up(2)
+    pair_in(1)
     down(2)
     pair_out(2)
+    ag.sib_in(1, 1)
     ag.sib_in(3, 1)
-    ag.sib_in(2, 1)
     gate_up(3)
     pair_in(2)
     down(3)
     pair_out(3)
+    relay(0, 2)
+    pair_in(3)
+    relay(1, 2)
+    y_sum(2)
+    x_sum(1)
     y_sum(1)
-    pair_in(3)
-    x_sum(1)
     y_sum(3)
-    y_sum(2)
+    relay(0, 0)
     y_sum(0)
     x_sum(0)
 
     def final(i, cols, srcs):
-        v = o_ref[0, :, cols].astype(f32)
-        for src in srcs:
-            v = v + src.astype(f32)
+        if srcs is None:
+            v = jnp.concatenate([sum_ref[0], sum_ref[1]], axis=1)
+        else:
+            v = o_ref[0, :, cols].astype(f32)
+            for src in srcs:
+                v = v + src.astype(f32)
         con_ref[:, cols] = lax.dot_general(
             sel, (v * gate_col).astype(bf16), (((0,), (0,)), ((), ())), preferred_element_type=f32
         ).astype(bf16)
@@ -634,11 +682,16 @@
             total = total + rec_ref[k - 1, :, cols].astype(f32)
         out_ref[:, cols] = total.astype(bf16)
 
-    mail.got(yq_ref, fsem.at[3], w.tok_dev(0, 1, 0))
+    mail.got(yq_ref, fsem.at[0], w.tok_dev(0, 1, 0))
     final(1, Q, [yq_ref[...]])
-    for b in range(3):
-        mail.got(xp_ref.at[b], fsem.at[b], w.tok_dev(1, 0, 0))
-    final(0, P, [xp_ref[b] for b in range(3)])
+    x_in(0, 0)
+    for p in (0, 1):
+        i = lot(0, p) * 2
+        add(
+            0, quarter[p], lambda r, i=i: xf_ref[i, r, :], lambda r, i=i: xf_ref[i + 1, r, :],
+            out=sum_ref.at[p],
+        )
+    final(0, P, None)
     finish(1, Q)
     finish(0, P)
     mail.drain()
@@ -650,7 +703,7 @@
     toks, cap = rows * NE, 80
     cut = model // 2
     vm = pl.BlockSpec(memory_space=pltpu.VMEM)
-    sends = 7 * (NE - 1) + AG_SENDS + 8 + 4 + 6 + 3 + 1
+    sends = 7 * (NE - 1) + AG_SENDS + 8 + 4 + 12 + 1 + 6
     dma = pltpu.SemaphoreType.DMA
     return pl.pallas_call(
         expert_kernel,
@@ -667,13 +720,14 @@
             pltpu.VMEM((8, cap, model), bf16),
             pltpu.VMEM((4, cap, cut), bf16),
             pltpu.VMEM((cap, model - cut), bf16),
-            pltpu.VMEM((3, cap, cut), bf16),
-            pltpu.VMEM((6, cap, model - cut), bf16),
+            pltpu.VMEM((12, cap, model // 4), bf16),
+            pltpu.VMEM((6, cap, model // 4), bf16),
+            pltpu.VMEM((2, cap, model // 4), f32),
             pltpu.VMEM((toks, model), bf16),
             pltpu.VMEM((NE - 1, rows, model), bf16),
             pltpu.VMEM((rows, 128), bf16),
             dma((3,)), dma((sends,)), dma((4, NE - 1)), dma((NE - 1,)), dma((16, 4)), dma((8,)),
-            dma((4,)), dma((6,)), dma((4,)), dma((2, NE - 1)),
+            dma((4,)), dma((12,)), dma((6,)), dma((1,)), dma((2, NE - 1)),
         ],
         compiler_params=pltpu.CompilerParams(
             collective_id=2, has_side_effects=True, vmem_limit_bytes=60 * 2**20
@@ -692,7 +746,7 @@
     hidden, normed = mixer(
         x_in, conv_w, b_proj, c_proj, log_decay.T, d_skip[None], w_out, norm_gain[None], rows
     )
-    layer_out = expert_layer(normed, route_ids[0], hidden, w_router.T, w_expert)
+    layer_out = expert_layer(normed, route_ids[0].T, hidden, w_router.T, w_expert)
     return layer_out.reshape(1, rows, model)
 
 

time: 188 us -> 178 us (0.947)
  Pallas kernels: 185 us -> 176 us
    pallas_call x1, Pallas kernels: 128 us -> 119 us  [expert_layer(): pl.pallas_call(expert_kernel, out_shape=jax.ShapeDtypeStruct((rows, model...]
where the time goes in v5:
time: 178 us; the launch traced here: 177 us
  Pallas kernels  176 us (99%)
    pallas_call x1, Pallas kernels, expert_layer(): pl.pallas_call(expert_kernel, out_shape=jax.ShapeDtypeStruct((rows, model...  119 us
    pallas_call x1, Pallas kernels, mixer(): pl.pallas_call(mixer_kernel, out_shape=[jax.ShapeDtypeStruct((rows, model...  56.9 us

profile of v5, /device:TPU:6, one launch (start us, length us, event | category | flops | bytes accessed | tf_op | source)
XLA Modules:
  0.0 177.4 jit_solution(12003198979081711903)
XLA Ops:
  0.0 56.9 %mixer.1 = (bf16[16,4096]{1,0:T(8,128)(2,1)}, bf16[16,4096]{1,0:T(8,128)(2,1)}) custom-call(bf16[128,1024]{1,0:T(8,128)(2,1)} %x_hbm.1, f32[4,1024]{1,0:T(4,128)} %cw_hbm.1, bf16[128,128]{1,0:T(8,128)(2,1)} %b_hbm.1, bf16[128,128]{1,0:T(8,128)(2,1)} %c_hbm.1, f32[16,128]{1,0:T(8,128)} %bitcast.11, f32[1,16]{1,0:T(1,128)} %bitcast.13, ...), custom_call_target="tpu_custom_call" | custom-call | flops 1073741824 | bytes 20971520 | tf_op jit(solution)/shard_map/mixer/pallas_call | solution.py:388
  56.9 118.9 %expert_layer.1 = bf16[16,4096]{1,0:T(8,128)(2,1)} custom-call(bf16[16,4096]{1,0:T(8,128)(2,1)} %get-tuple-element.7.nrm_ref, s32[2,16]{1,0:T(2,128)} %bitcast.12, bf16[16,4096]{1,0:T(8,128)(2,1)} %get-tuple-element.8.hid_ref, bf16[8,4096]{1,0:T(8,128)(2,1)} %bitcast.9, bf16[1,3,4096,768]{3,2,1,0:T(8,128)(2,1)} %we_ref.1), custom_call_target="tpu_custom_call" | custom-call | flops 24159191040 | bytes 20971520 | tf_op jit(solution)/shard_map/expert_layer/pallas_call | solution.py:708
  175.8 1.6 copy.13
